TPU v7x, 128 devices: a whole 4x4x4 slice. The times are simulated.
128 devices in a mesh: row: 8 (over x, core), col: 16 (over y, z).
Axes of the slice: x: 4, y: 4, z: 4, core: 2. Of those that a mesh axis runs over, the one named last changes fastest.
Arguments:
- panel: float32 [8192, 512], P(('row', 'col')), as said below
- trailing: float32 [8192, 32768], P('row', 'col'), may hold values from -6 to 6
Outputs:
- r_factor: float32 [512, 512], replicated
- coupling: float32 [512, 32768], P(None, 'col')
- trailing_out: float32 [8192, 32768], P('row', 'col')
Inputs may be any that keep to these rules, and one draw needn't show every extreme that they name: The panel has full column rank with moderate conditioning; its rows carry scales that differ, and its columns share a common component.
All inputs are finite; a program needn't handle non-finite values.
Results may differ from a plain program's by a relative error of at most 0.000086.
Values sent between devices are 32-bit elements; how exact they have to be, the bound alone decides.
No kernel may reach another device: no remote copies, remote signals or barrier semaphores. Data moves between devices by JAX's collectives and lax.ppermute only.
A program may use at most 128 MiB of HBM per device.

v0:
```python
import functools

import jax
import jax.numpy as jnp
from jax import lax
from jax.experimental import pallas as pl
from jax.experimental.pallas import tpu as pltpu
from jax.sharding import PartitionSpec as P

HIGHEST = lax.Precision.HIGHEST
BF16 = jnp.bfloat16
F32 = jnp.float32
GROUP = 32
TILE = 512


def near(i):
    return i ^ 1


def far(i):
    return 3 - i


CORE = [(r, r ^ 1) for r in range(8)]
XPAIR = [[(x * 2 + c, pair(x) * 2 + c) for x in range(4) for c in range(2)] for pair in (near, far)]
YPAIR = [[(y * 4 + z, pair(y) * 4 + z) for y in range(4) for z in range(4)] for pair in (near, far)]
ZPAIR = [[(y * 4 + z, y * 4 + pair(z)) for y in range(4) for z in range(4)] for pair in (near, far)]


def ring_bits(i):
    return (i ^ (i // 2)) & 1, i // 2


def tdot(a, b, precision=HIGHEST):
    return lax.dot_general(a, b, (((0,), (0,)), ((), ())), precision=precision, preferred_element_type=F32)


def spread(v, s):
    return jnp.broadcast_to(v[s:s + 1, :], (8, 128))


def eliminate(slab, off, g):
    nt = g // 8
    width = slab.shape[1] // 128
    sub = lax.broadcasted_iota(jnp.int32, (8, 128), 0)
    rows = [[slab[8 * t:8 * t + 8, 128 * w:128 * w + 128] for w in range(width)] for t in range(nt)]
    cols = [
        [jnp.broadcast_to(rows[t][0][:, off + k:off + k + 1], (8, 128)) if t >= k // 8 else None for t in range(nt)]
        for k in range(g)
    ]
    scale = [None] * nt
    for j in range(g):
        tj, sj = divmod(j, 8)
        d = spread(cols[j][tj], sj)
        inv = 1.0 / d
        root = lax.rsqrt(d)
        scale[tj] = root if sj == 0 else jnp.where(sub >= sj, root, scale[tj])
        f = [None if t < tj else cols[j][t] * inv for t in range(nt)]
        for k in range(j + 1, g):
            a = spread(cols[j][k // 8], k % 8)
            for t in range(k // 8, nt):
                cols[k][t] = cols[k][t] - f[t] * a
        f[tj] = jnp.where(sub > sj, f[tj], 0.0)
        for w in range(width):
            p = spread(rows[tj][w], sj)
            for t in range(tj, nt):
                if t > tj or sj < 7:
                    rows[t][w] = rows[t][w] - f[t] * p
    return jnp.concatenate(
        [jnp.concatenate([rows[t][w] * scale[t] for w in range(width)], axis=1) for t in range(nt)], axis=0
    )


def params(mib=40):
    return pltpu.CompilerParams(vmem_limit_bytes=mib << 20)


def whole(n=1):
    return [pl.BlockSpec(memory_space=pltpu.VMEM)] * n


SCALARS = pl.BlockSpec(memory_space=pltpu.SMEM)


def split(a):
    high = a.astype(BF16)
    return high, (a - high.astype(F32)).astype(BF16)


def dot(a, b):
    return jnp.dot(a, b, preferred_element_type=F32)


def dot3(a, b):
    return dot(a[0], b[0]) + (dot(a[0], b[1]) + dot(a[1], b[0]))


def factor_kernel(k, nb, *refs):
    earlier, g_ref, w, m = refs[:k], refs[k], refs[k + 1], refs[k + 2]
    first = sum(nb - i for i in range(k)) * 128
    for j in range(nb - k):
        m[:, j * 128:j * 128 + 128] = g_ref[first + j * 128:first + j * 128 + 128, :]
    if k:
        m[:, (nb - k) * 128:nb * 128] = jnp.zeros((128, k * 128), F32)
    ri = lax.broadcasted_iota(jnp.int32, (128, 128), 0)
    ci = lax.broadcasted_iota(jnp.int32, (128, 128), 1)
    m[:, nb * 128:] = jnp.where(ri == ci, 1.0, 0.0)
    for i in range(k):
        at = (k - i) * 128
        known = earlier[i][:, at:]
        width = known.shape[1]
        m[:, :width] = m[:, :width] - tdot(earlier[i][:, at:at + 128], known)
    for q in range(128 // GROUP):
        lo, hi = q * GROUP, (q + 1) * GROUP
        slab = m[lo:hi, :]
        if q:
            slab = slab - tdot(w[0:lo, lo:hi], w[0:lo, :])
        w[lo:hi, :] = eliminate(slab, lo, GROUP)


def factor_rows(k, nb, earlier, packed):
    window = (nb + 1) * 128
    return pl.pallas_call(
        functools.partial(factor_kernel, k, nb),
        out_shape=jax.ShapeDtypeStruct((128, window), F32),
        in_specs=whole(k + 1),
        out_specs=whole()[0],
        scratch_shapes=[pltpu.VMEM((128, window), F32)],
        compiler_params=params(16),
        cost_estimate=pl.CostEstimate(flops=5 * 10 ** 9, bytes_accessed=18 * 10 ** 6, transcendentals=0),
        name="factor",
    )(*earlier, packed)


def gram_kernel(order_ref, a0, a1, a2, a3, o_ref, keep_ref, give_ref, blocks):
    for q, ref in enumerate((a0, a1, a2, a3)):
        for p in range(16):
            at = pl.multiple_of(order_ref[q * 16 + p] * 64, 64)
            o_ref[pl.ds(at, 64), q * 128:q * 128 + 128] = ref[p * 64:p * 64 + 64, :]
    at = 0
    for i in range(4):
        strip = tdot(o_ref[:, i * 128:i * 128 + 128], o_ref[:, i * 128:])
        for j in range(4 - i):
            blocks[at:at + 128, :] = strip[:, j * 128:j * 128 + 128]
            at += 128
    core = order_ref[64]
    keep_ref[...] = blocks[pl.ds(pl.multiple_of(core * 640, 128), 640), :]
    give_ref[...] = blocks[pl.ds(pl.multiple_of((1 - core) * 640, 128), 640), :]


def gather_panel(panel, core):
    col = lax.axis_index("col")
    y, z = col // 4, col % 4
    pairs = {"y": YPAIR, "z": ZPAIR}
    orders = (
        (("z", 0), ("z", 1), ("y", 0), ("y", 1)),
        (("z", 1), ("z", 0), ("y", 1), ("y", 0)),
        (("y", 0), ("y", 1), ("z", 0), ("z", 1)),
        (("y", 1), ("y", 0), ("z", 1), ("z", 0)),
    )
    held = [panel[:, q * 128:q * 128 + 128] for q in range(4)]
    where = [[(y, z)] for _ in range(4)]
    flip = (near, far)
    for step in range(4):
        got = []
        for q in range(4):
            axis, side = orders[q][step]
            got.append(lax.ppermute(held[q], "col", pairs[axis][side]))
        for q in range(4):
            axis, side = orders[q][step]
            held[q] = jnp.concatenate([held[q], got[q]], axis=0)
            other = [(flip[side](a), b) if axis == "y" else (a, flip[side](b)) for a, b in where[q]]
            where[q] = where[q] + other
    table = jnp.stack([a * 4 + b for q in range(4) for a, b in where[q]] + [core]).astype(jnp.int32)
    half = jax.ShapeDtypeStruct((640, 128), F32)
    return pl.pallas_call(
        gram_kernel,
        out_shape=(jax.ShapeDtypeStruct((1024, 512), F32), half, half),
        in_specs=[SCALARS] + whole(4),
        out_specs=whole(3),
        scratch_shapes=[pltpu.VMEM((1280, 128), F32)],
        compiler_params=params(),
        name="gram",
    )(table, *held)


def join(own, other, bit):
    first = bit == 0
    return jnp.concatenate([jnp.where(first, own, other), jnp.where(first, other, own)], axis=0)


def swap(a, pairs):
    return lax.ppermute(a, "row", pairs)


def sum_packed(keep, give, core):
    a = keep + swap(give, CORE)
    n = a.shape[0] // 2
    one, two = a[:n], a[n:]
    for side in (0, 1):
        one, two = one + swap(one, XPAIR[side]), two + swap(two, XPAIR[1 - side])
    a = jnp.concatenate([one, two], axis=0)
    return join(a, swap(a, CORE), core)


def turn_kernel(p_ref, hi_ref, lo_ref):
    for j in range(0, 1024, 128):
        hi_ref[:, j:j + 128], lo_ref[:, j:j + 128] = split(jnp.transpose(p_ref[j:j + 128, :]))


def turn(rows):
    out = jax.ShapeDtypeStruct((rows.shape[1], rows.shape[0]), BF16)
    return pl.pallas_call(
        turn_kernel, out_shape=(out, out), in_specs=whole(), out_specs=whole(2), compiler_params=params(), name="turn"
    )(rows)


def share_kernel(table_ref, hi_ref, lo_ref, t_ref, o_ref):
    rows = pl.ds(pl.multiple_of(table_ref[0] * 256, 256), 256)
    got = dot3((hi_ref[rows, :], lo_ref[rows, :]), split(t_ref[...]))
    for p in range(8):
        at = pl.multiple_of(table_ref[1 + p] * 32, 32)
        o_ref[pl.ds(at, 32), :] = got[p * 32:p * 32 + 32, :]


def share(table, hi, lo, trailing):
    depth, width = trailing.shape
    return pl.pallas_call(
        share_kernel,
        out_shape=jax.ShapeDtypeStruct((256, width), F32),
        grid=(width // TILE,),
        in_specs=[SCALARS] + whole(2) + [pl.BlockSpec((depth, TILE), lambda i: (0, i))],
        out_specs=pl.BlockSpec((256, TILE), lambda i: (0, i)),
        compiler_params=params(),
        cost_estimate=pl.CostEstimate(flops=3 * 10 ** 9, bytes_accessed=12 * 10 ** 6, transcendentals=0),
        name="share",
    )(table, hi, lo, trailing)


def prepare_kernel(w0, w1, w2, w3, p_ref, r_ref, ihi_ref, ilo_ref, bhi_ref, blo_ref, inv):
    ri = lax.broadcasted_iota(jnp.int32, (128, 128), 0)
    ci = lax.broadcasted_iota(jnp.int32, (128, 128), 1)
    zero = jnp.zeros((128, 128), F32)
    for i, w in enumerate((w0, w1, w2, w3)):
        rows = slice(i * 128, i * 128 + 128)
        for j in range(4):
            cols = slice(j * 128, j * 128 + 128)
            if j < i:
                r_ref[rows, cols] = zero
            else:
                block = w[:, (j - i) * 128:(j - i) * 128 + 128]
                r_ref[rows, cols] = jnp.where(ri <= ci, block, 0.0) if j == i else block
            inv[rows, cols] = w[:, (4 - i + j) * 128:(5 - i + j) * 128] if j <= i else zero
    ihi_ref[...], ilo_ref[...] = split(inv[...])
    turned = split(jnp.transpose(inv[...]))
    for at in range(0, 1024, 256):
        rows = slice(at, at + 256)
        bhi_ref[rows, :], blo_ref[rows, :] = split(dot3(split(p_ref[rows, :]), turned))


def prepare(factors, rows):
    b = rows.shape[1]
    square, tall = (b, b), rows.shape
    return pl.pallas_call(
        prepare_kernel,
        out_shape=[jax.ShapeDtypeStruct(s, t) for s, t in ((square, F32), (square, BF16), (square, BF16), (tall, BF16), (tall, BF16))],
        in_specs=whole(5),
        out_specs=whole(5),
        scratch_shapes=[pltpu.VMEM(square, F32)],
        compiler_params=params(),
        cost_estimate=pl.CostEstimate(flops=3 * 10 ** 9, bytes_accessed=10 * 10 ** 6, transcendentals=0),
        name="prepare",
    )(*factors, rows)


def finish_kernel(table_ref, *refs):
    pieces, (ihi, ilo, bhi, blo, t_ref, c_ref, o_ref, total) = refs[:8], refs[8:]
    for p in range(8):
        for half in (0, 1):
            at = pl.multiple_of(table_ref[2 * p + half] * 32, 32)
            total[pl.ds(at, 32), :] = pieces[p][half * 32:half * 32 + 32, :]
    coupling = dot3((ihi[...], ilo[...]), split(total[...]))
    c_ref[...] = coupling
    c = split(coupling)
    for at in range(0, 1024, 256):
        rows = slice(at, at + 256)
        o_ref[rows, :] = t_ref[rows, :] - dot3((bhi[rows, :], blo[rows, :]), c)


def finish(table, pieces, ihi, ilo, bhi, blo, trailing):
    depth, width = trailing.shape
    b = ihi.shape[0]
    return pl.pallas_call(
        finish_kernel,
        out_shape=(jax.ShapeDtypeStruct((b, width), F32), jax.ShapeDtypeStruct((depth, width), F32)),
        grid=(width // TILE,),
        in_specs=[SCALARS]
        + [pl.BlockSpec((64, TILE), lambda i: (0, i))] * 8
        + whole(4)
        + [pl.BlockSpec((depth, TILE), lambda i: (0, i))],
        out_specs=(pl.BlockSpec((b, TILE), lambda i: (0, i)), pl.BlockSpec((depth, TILE), lambda i: (0, i))),
        scratch_shapes=[pltpu.VMEM((b, TILE), F32)],
        compiler_params=params(48),
        name="finish",
    )(table, *pieces, ihi, ilo, bhi, blo, trailing)


def local(panel, trailing):
    row = lax.axis_index("row")
    core = row % 2
    bits = ring_bits(row // 2)
    rows, keep, give = gather_panel(panel, core)
    packed = sum_packed(keep, give, core)
    hi, lo = turn(rows)

    def held(part, i, j):
        s, t = (bits[0], bits[1]) if part == 0 else (bits[1], bits[0])
        return part * 4 + (i ^ s) * 2 + (j ^ t)

    spots = [held(part, i, j) for part in (0, 1) for i in (0, 1) for j in (0, 1)]
    give = share(jnp.stack([1 - core] + spots).astype(jnp.int32), hi, lo, trailing)
    keep = share(jnp.stack([core] + spots).astype(jnp.int32), hi, lo, trailing)
    got = swap(give, CORE)
    parts = [[keep[at:at + 64] + got[at:at + 64], keep[at + 64:at + 128] + got[at + 64:at + 128]] for at in (0, 128)]
    came = [swap(parts[h][1], XPAIR[h]) for h in (0, 1)]
    parts = [[parts[h][0][:32] + came[h][:32], parts[h][0][32:] + came[h][32:]] for h in (0, 1)]

    factors = [factor_rows(0, 4, [], packed)]
    factors.append(factor_rows(1, 4, factors, packed))
    parts, factors = lax.optimization_barrier((parts, factors))
    came = [swap(parts[h][1], XPAIR[1 - h]) for h in (0, 1)]
    own = [parts[h][0] + came[h] for h in (0, 1)]
    factors.append(factor_rows(2, 4, factors, packed))
    own, factors = lax.optimization_barrier((own, factors))
    came = [swap(own[h], XPAIR[1 - h]) for h in (0, 1)]
    own = [jnp.concatenate([own[h], came[h]], axis=0) for h in (0, 1)]
    factors.append(factor_rows(3, 4, factors, packed))
    own, factors = lax.optimization_barrier((own, factors))
    came = [swap(own[h], XPAIR[h]) for h in (0, 1)]
    r_factor, ihi, ilo, bhi, blo = prepare(factors, rows)
    mine = [own[0], came[0], own[1], came[1]]
    theirs = [swap(p, CORE) for p in mine]
    spots = [c * 8 + s for c in (core, 1 - core) for s in spots]
    coupling, out = finish(jnp.stack(spots).astype(jnp.int32), mine + theirs, ihi, ilo, bhi, blo, trailing)
    return (r_factor, coupling, out)


def solution(mesh):
    placed = (P(("row", "col"), None), P("row", "col"))
    return jax.shard_map(
        local,
        mesh=mesh,
        in_specs=placed,
        out_specs=(P(), P(None, "col"), P("row", "col")),
        check_vma=False,
    )
```

profile of v0, /device:TPU:1, one launch (start us, length us, event | category | flops | bytes accessed | tf_op | source)
XLA Modules:
  0.0 151.4 jit_solution(3569071803008571666)
XLA Ops:
  0.6 0.8 fusion.1
  1.5 3.6 %collective-permute-start.12 = (f32[64,128]{1,0:T(8,128)S(1)}, f32[64,128]{1,0:T(8,128)S(1)}, u32[]{:S(2)}, u32[]{:S(2)}) collective-permute-start(f32[64,128]{1,0:T(8,128)S(1)} %get-tuple-element.75), channel_id=1, source_target_pairs={{0,12},{1,13},{2,14},{3,15},{4,8},{5,9},{6,10},{7,11},{8,4},{9,5},... | collective-permute-start | bytes 98312 | tf_op jit(solution)/shard_map/ppermute | solution.py:169
  5.1 3.8 %collective-permute-start.4 = (f32[64,128]{1,0:T(8,128)S(1)}, f32[64,128]{1,0:T(8,128)S(1)}, u32[]{:S(2)}, u32[]{:S(2)}) collective-permute-start(f32[64,128]{1,0:T(8,128)S(1)} %get-tuple-element.80), channel_id=1, source_target_pairs={{0,3},{1,2},{2,1},{3,0},{4,7},{5,6},{6,5},{7,4},{8,11},{9,10},{10,... | collective-permute-start | bytes 98312 | tf_op jit(solution)/shard_map/ppermute | solution.py:169
  9.1 1.5 %collective-permute-start.13 = (f32[128,128]{1,0:T(8,128)S(1)}, f32[128,128]{1,0:T(8,128)S(1)}, u32[]{:S(2)}, u32[]{:S(2)}) collective-permute-start(f32[128,128]{1,0:T(8,128)S(1)} %pad_maximum_fusion.15), channel_id=1, source_target_pairs={{0,4},{1,5},{2,6},{3,7},{4,0},{5,1},{6,2},{7,3},{8,12},{9,13},{10,... | collective-permute-start | bytes 196616 | tf_op jit(solution)/shard_map/ppermute | solution.py:169
  10.7 1.5 %collective-permute-start.5 = (f32[128,128]{1,0:T(8,128)S(1)}, f32[128,128]{1,0:T(8,128)S(1)}, u32[]{:S(2)}, u32[]{:S(2)}) collective-permute-start(f32[128,128]{1,0:T(8,128)S(1)} %pad_maximum_fusion.13), channel_id=1, source_target_pairs={{0,1},{1,0},{2,3},{3,2},{4,5},{5,4},{6,7},{7,6},{8,9},{9,8},{10,11... | collective-permute-start | bytes 196616 | tf_op jit(solution)/shard_map/ppermute | solution.py:169
  13.3 2.0 %collective-permute-start.14 = (f32[256,128]{1,0:T(8,128)S(1)}, f32[256,128]{1,0:T(8,128)S(1)}, u32[]{:S(2)}, u32[]{:S(2)}) collective-permute-start(f32[256,128]{1,0:T(8,128)S(1)} %pad_maximum_fusion.11), channel_id=1, source_target_pairs={{0,3},{1,2},{2,1},{3,0},{4,7},{5,6},{6,5},{7,4},{8,11},{9,10},{10,... | collective-permute-start | bytes 393224 | tf_op jit(solution)/shard_map/ppermute | solution.py:169
  15.3 2.7 %collective-permute-start.6 = (f32[256,128]{1,0:T(8,128)S(1)}, f32[256,128]{1,0:T(8,128)S(1)}, u32[]{:S(2)}, u32[]{:S(2)}) collective-permute-start(f32[256,128]{1,0:T(8,128)S(1)} %pad_maximum_fusion.9), channel_id=1, source_target_pairs={{0,12},{1,13},{2,14},{3,15},{4,8},{5,9},{6,10},{7,11},{8,4},{9,5},... | collective-permute-start | bytes 393224 | tf_op jit(solution)/shard_map/ppermute | solution.py:169
  18.4 3.7 %collective-permute-done.10 = f32[256,128]{1,0:T(8,128)S(1)} collective-permute-done((f32[256,128]{1,0:T(8,128)S(1)}, f32[256,128]{1,0:T(8,128)S(1)}, u32[]{:S(2)}, u32[]{:S(2)}) %collective-permute-start.10) | collective-permute-done | bytes 131104 | tf_op jit(solution)/shard_map/ppermute | solution.py:169
  22.1 1.9 %collective-permute-start.11 = (f32[512,128]{1,0:T(8,128)S(1)}, f32[512,128]{1,0:T(8,128)S(1)}, u32[]{:S(2)}, u32[]{:S(2)}) collective-permute-start(f32[512,128]{1,0:T(8,128)S(1)} %pad_maximum_fusion.6), channel_id=1, source_target_pairs={{0,3},{1,2},{2,1},{3,0},{4,7},{5,6},{6,5},{7,4},{8,11},{9,10},{10,... | collective-permute-start | bytes 786440 | tf_op jit(solution)/shard_map/ppermute | solution.py:169
  25.0 3.6 %collective-permute-done.11 = f32[512,128]{1,0:T(8,128)S(1)} collective-permute-done((f32[512,128]{1,0:T(8,128)S(1)}, f32[512,128]{1,0:T(8,128)S(1)}, u32[]{:S(2)}, u32[]{:S(2)}) %collective-permute-start.11) | collective-permute-done | bytes 262176 | tf_op jit(solution)/shard_map/ppermute | solution.py:169
  28.6 2.0 %collective-permute-done.3 = f32[512,128]{1,0:T(8,128)S(1)} collective-permute-done((f32[512,128]{1,0:T(8,128)S(1)}, f32[512,128]{1,0:T(8,128)S(1)}, u32[]{:S(2)}, u32[]{:S(2)}) %collective-permute-start.3) | collective-permute-done | bytes 262176 | tf_op jit(solution)/shard_map/ppermute | solution.py:169
  30.7 4.1 %gram.1 = (f32[1024,512]{1,0:T(8,128)S(1)}, f32[640,128]{1,0:T(8,128)S(1)}, f32[640,128]{1,0:T(8,128)S(1)}) custom-call(s32[65]{0:T(128)S(1)} %stack.242.order_ref, f32[1024,128]{1,0:T(8,128)S(1)} %constant_dynamic-update-slice_fusion.a0, f32[1024,128]{1,0:T(8,128)S(1)} %constant_dynamic-update-slice_fusion.5.a1, ...), custom_call_target="tpu_custom_call" | custom-call | tf_op jit(solution)/shard_map/gram/pallas_call | solution.py:177
  35.5 5.8 %share.3 = f32[256,2048]{1,0:T(8,128)} custom-call(s32[9]{0:T(128)S(1)} %stack.244.table_ref, bf16[512,1024]{1,0:T(8,128)(2,1)S(1)} %get-tuple-element.33.hi_ref, bf16[512,1024]{1,0:T(8,128)(2,1)S(1)} %get-tuple-element.34.lo_ref, f32[1024,2048]{1,0:T(8,128)S(1)} %copy-done), custom_call_target="tpu_custom_call" | custom-call | flops 3000000000 | bytes 12000000 | tf_op jit(solution)/shard_map/share/pallas_call | solution.py:229
  41.3 5.8 %collective-permute-start.16 = (f32[256,2048]{1,0:T(8,128)}, f32[256,2048]{1,0:T(8,128)}, u32[]{:S(2)}, u32[]{:S(2)}) collective-permute-start(f32[256,2048]{1,0:T(8,128)} %share.3), channel_id=1, source_target_pairs={{0,16},{16,0},{32,48},{48,32},{64,80},{80,64},{96,112},{112,96},{1... | collective-permute-start | bytes 6291464 | tf_op jit(solution)/shard_map/ppermute | solution.py:194
  47.1 4.1 %collective-permute-done.19 = f32[640,128]{1,0:T(8,128)S(1)} collective-permute-done((f32[640,128]{1,0:T(8,128)S(1)}, f32[640,128]{1,0:T(8,128)S(1)}, u32[]{:S(2)}, u32[]{:S(2)}) %collective-permute-start.19) | collective-permute-done | bytes 327712 | tf_op jit(solution)/shard_map/ppermute | solution.py:194
  51.3 1.3 collective-permute-start.20
  52.6 1.8 %collective-permute-start.22 = (f32[320,128]{1,0:T(8,128)S(1)}, f32[320,128]{1,0:T(8,128)S(1)}, u32[]{:S(2)}, u32[]{:S(2)}) collective-permute-start(f32[320,128]{1,0:T(8,128)S(1)} %get-tuple-element.74), channel_id=1, source_target_pairs={{0,96},{16,112},{32,64},{48,80},{64,32},{80,48},{96,0},{112,16},{1... | collective-permute-start | bytes 491528 | tf_op jit(solution)/shard_map/ppermute | solution.py:194
  54.4 2.6 %collective-permute-done.20 = f32[320,128]{1,0:T(8,128)S(1)} collective-permute-done((f32[320,128]{1,0:T(8,128)S(1)}, f32[320,128]{1,0:T(8,128)S(1)}, u32[]{:S(2)}, u32[]{:S(2)}) %collective-permute-start.20) | collective-permute-done | bytes 163872 | tf_op jit(solution)/shard_map/ppermute | solution.py:194
  57.0 2.1 %collective-permute-done.22 = f32[320,128]{1,0:T(8,128)S(1)} collective-permute-done((f32[320,128]{1,0:T(8,128)S(1)}, f32[320,128]{1,0:T(8,128)S(1)}, u32[]{:S(2)}, u32[]{:S(2)}) %collective-permute-start.22) | collective-permute-done | bytes 163872 | tf_op jit(solution)/shard_map/ppermute | solution.py:194
  59.1 1.9 %collective-permute-start.21 = (f32[320,128]{1,0:T(8,128)S(1)}, f32[320,128]{1,0:T(8,128)S(1)}, u32[]{:S(2)}, u32[]{:S(2)}) collective-permute-start(f32[320,128]{1,0:T(8,128)S(1)} %get-tuple-element.71), channel_id=1, source_target_pairs={{0,96},{16,112},{32,64},{48,80},{64,32},{80,48},{96,0},{112,16},{1... | collective-permute-start | bytes 491528 | tf_op jit(solution)/shard_map/ppermute | solution.py:194
  61.0 3.6 %collective-permute-done.21 = f32[320,128]{1,0:T(8,128)S(1)} collective-permute-done((f32[320,128]{1,0:T(8,128)S(1)}, f32[320,128]{1,0:T(8,128)S(1)}, u32[]{:S(2)}, u32[]{:S(2)}) %collective-permute-start.21) | collective-permute-done | bytes 163872 | tf_op jit(solution)/shard_map/ppermute | solution.py:194
  64.6 0.9 collective-permute-done.23
  65.6 2.5 %collective-permute-start.24 = (f32[640,128]{1,0:T(8,128)S(1)}, f32[640,128]{1,0:T(8,128)S(1)}, u32[]{:S(2)}, u32[]{:S(2)}) collective-permute-start(f32[640,128]{1,0:T(8,128)S(1)} %pad_maximum_fusion.3), channel_id=1, source_target_pairs={{0,16},{16,0},{32,48},{48,32},{64,80},{80,64},{96,112},{112,96},{1... | collective-permute-start | bytes 983048 | tf_op jit(solution)/shard_map/ppermute | solution.py:194
  68.1 3.4 %copy-done.1 = f32[1024,2048]{1,0:T(8,128)S(1)} copy-done((f32[1024,2048]{1,0:T(8,128)S(1)}, f32[1024,2048]{1,0:T(8,128)}, u32[]{:S(2)}) %copy-start.1) | copy-done | bytes 8388632
  71.5 5.1 %share.2 = f32[256,2048]{1,0:T(8,128)S(1)} custom-call(s32[9]{0:T(128)S(1)} %stack.218.table_ref, bf16[512,1024]{1,0:T(8,128)(2,1)S(1)} %get-tuple-element.33.hi_ref, bf16[512,1024]{1,0:T(8,128)(2,1)S(1)} %get-tuple-element.34.lo_ref, f32[1024,2048]{1,0:T(8,128)S(1)} %copy-done.1), custom_call_target="tpu_custom_call" | custom-call | flops 3000000000 | bytes 12000000 | tf_op jit(solution)/shard_map/share/pallas_call | solution.py:229
  76.8 1.9 %slice_add_fusion.1 = (f32[64,2048]{1,0:T(8,128)S(1)}, f32[64,2048]{1,0:T(8,128)S(1)}, f32[64,2048]{1,0:T(8,128)S(1)}, f32[64,2048]{1,0:T(8,128)S(1)}) fusion(f32[256,2048]{1,0:T(8,128)} %collective-permute-done.16, f32[256,2048]{1,0:T(8,128)S(1)} %share.2), kind=kLoop, calls=%fused_computation.2 | loop fusion | flops 524288 | bytes 6291456 | tf_op jit(solution)/shard_map/add | solution.py:325
  78.6 1.1 collective-permute-start.18
  79.7 3.6 %factor.4.refs_0_.w0 = f32[128,640]{1,0:T(8,128)S(1)} custom-call(f32[1280,128]{1,0:T(8,128)S(1)} %pad_maximum_fusion.refs_0_.refs_1_.refs_2_.refs_3_), custom_call_target="tpu_custom_call" | custom-call | flops 5000000000 | bytes 18000000 | tf_op jit(solution)/shard_map/factor/pallas_call | solution.py:124
  83.4 4.0 %factor.5.refs_1_.w1 = f32[128,640]{1,0:T(8,128)S(1)} custom-call(f32[128,640]{1,0:T(8,128)S(1)} %factor.4.refs_0_.w0, f32[1280,128]{1,0:T(8,128)S(1)} %pad_maximum_fusion.refs_0_.refs_1_.refs_2_.refs_3_), custom_call_target="tpu_custom_call" | custom-call | flops 5000000000 | bytes 18000000 | tf_op jit(solution)/shard_map/factor/pallas_call | solution.py:124
  87.5 6.0 %collective-permute-done.18 = f32[64,2048]{1,0:T(8,128)S(1)} collective-permute-done((f32[64,2048]{1,0:T(8,128)S(1)}, f32[64,2048]{1,0:T(8,128)S(1)}, u32[]{:S(2)}, u32[]{:S(2)}) %collective-permute-start.18) | collective-permute-done | bytes 524320 | tf_op jit(solution)/shard_map/ppermute | solution.py:194
  93.5 3.1 %collective-permute-done.17 = f32[64,2048]{1,0:T(8,128)S(1)} collective-permute-done((f32[64,2048]{1,0:T(8,128)S(1)}, f32[64,2048]{1,0:T(8,128)S(1)}, u32[]{:S(2)}, u32[]{:S(2)}) %collective-permute-start.17) | collective-permute-done | bytes 524320 | tf_op jit(solution)/shard_map/ppermute | solution.py:194
  96.7 1.8 %collective-permute-start.25 = (f32[32,2048]{1,0:T(8,128)S(1)}, f32[32,2048]{1,0:T(8,128)S(1)}, u32[]{:S(2)}, u32[]{:S(2)}) collective-permute-start(f32[32,2048]{1,0:T(8,128)S(1)} %get-tuple-element.38), channel_id=1, source_target_pairs={{0,96},{16,112},{32,64},{48,80},{64,32},{80,48},{96,0},{112,16},{1... | collective-permute-start | bytes 786440 | tf_op jit(solution)/shard_map/ppermute | solution.py:194
  98.5 4.1 %factor.6.refs_2_.w2 = f32[128,640]{1,0:T(8,128)S(1)} custom-call(f32[128,640]{1,0:T(8,128)S(1)} %factor.4.refs_0_.w0, f32[128,640]{1,0:T(8,128)S(1)} %factor.5.refs_1_.w1, f32[1280,128]{1,0:T(8,128)S(1)} %pad_maximum_fusion.refs_0_.refs_1_.refs_2_.refs_3_), custom_call_target="tpu_custom_call" | custom-call | flops 5000000000 | bytes 18000000 | tf_op jit(solution)/shard_map/factor/pallas_call | solution.py:124
  102.6 2.1 %collective-permute-done.25 = f32[32,2048]{1,0:T(8,128)S(1)} collective-permute-done((f32[32,2048]{1,0:T(8,128)S(1)}, f32[32,2048]{1,0:T(8,128)S(1)}, u32[]{:S(2)}, u32[]{:S(2)}) %collective-permute-start.25) | collective-permute-done | bytes 262176 | tf_op jit(solution)/shard_map/ppermute | solution.py:194
  104.9 1.6 %collective-permute-start.27 = (f32[32,2048]{1,0:T(8,128)S(1)}, f32[32,2048]{1,0:T(8,128)S(1)}, u32[]{:S(2)}, u32[]{:S(2)}) collective-permute-start(f32[32,2048]{1,0:T(8,128)S(1)} %add.293), channel_id=1, source_target_pairs={{0,96},{16,112},{32,64},{48,80},{64,32},{80,48},{96,0},{112,16},{1... | collective-permute-start | bytes 786440 | tf_op jit(solution)/shard_map/ppermute | solution.py:194
  106.5 4.2 %factor.7.w3 = f32[128,640]{1,0:T(8,128)S(1)} custom-call(f32[128,640]{1,0:T(8,128)S(1)} %factor.4.refs_0_.w0, f32[128,640]{1,0:T(8,128)S(1)} %factor.5.refs_1_.w1, f32[128,640]{1,0:T(8,128)S(1)} %factor.6.refs_2_.w2, f32[1280,128]{1,0:T(8,128)S(1)} %pad_maximum_fusion.refs_0_.refs_1_.refs_2_.refs_3_), custom_call_target="tpu_custom_call" | custom-call | flops 5000000000 | bytes 18000000 | tf_op jit(solution)/shard_map/factor/pallas_call | solution.py:124
  112.4 1.3 collective-permute-start.30
  113.7 3.4 %collective-permute-start.31 = (f32[64,2048]{1,0:T(8,128)S(1)}, f32[64,2048]{1,0:T(8,128)}, u32[]{:S(2)}, u32[]{:S(2)}) collective-permute-start(f32[64,2048]{1,0:T(8,128)S(1)} %pad_maximum_fusion.1.refs_0_), channel_id=1, source_target_pairs={{0,16},{16,0},{32,48},{48,32},{64,80},{80,64},{96,112},{112,96},{1... | collective-permute-start | bytes 1572872 | tf_op jit(solution)/shard_map/ppermute | solution.py:194
  117.1 5.3 %collective-permute-done.29.refs_1_ = f32[64,2048]{1,0:T(8,128)} collective-permute-done((f32[64,2048]{1,0:T(8,128)S(1)}, f32[64,2048]{1,0:T(8,128)}, u32[]{:S(2)}, u32[]{:S(2)}) %collective-permute-start.29) | collective-permute-done | bytes 524320 | tf_op jit(solution)/shard_map/ppermute | solution.py:194
  122.5 4.1 %collective-permute-start.32 = (f32[64,2048]{1,0:T(8,128)}, f32[64,2048]{1,0:T(8,128)}, u32[]{:S(2)}, u32[]{:S(2)}) collective-permute-start(f32[64,2048]{1,0:T(8,128)} %collective-permute-done.29.refs_1_), channel_id=1, source_target_pairs={{0,16},{16,0},{32,48},{48,32},{64,80},{80,64},{96,112},{112,96},{1... | collective-permute-start | bytes 1572872 | tf_op jit(solution)/shard_map/ppermute | solution.py:194
  126.6 1.5 collective-permute-start.34
  128.2 1.0 copy-done.7
  129.2 1.0 copy-done.9
  130.1 1.0 copy-done.11
  131.1 3.0 %prepare.1 = (f32[512,512]{1,0:T(8,128)}, bf16[512,512]{1,0:T(8,128)(2,1)S(1)}, bf16[512,512]{1,0:T(8,128)(2,1)S(1)}, bf16[1024,512]{1,0:T(8,128)(2,1)S(1)}, bf16[1024,512]{1,0:T(8,128)(2,1)S(1)}) custom-call(f32[128,640]{1,0:T(8,128)S(1)} %factor.4.refs_0_.w0, f32[128,640]{1,0:T(8,128)S(1)} %copy-done.7, f32[128,640]{1,0:T(8,128)S(1)} %copy-done.9, ...), custom_call_target="tpu_custom_call" | custom-call | flops 3000000000 | bytes 10000000 | tf_op jit(solution)/shard_map/prepare/pallas_call | solution.py:265
  134.1 1.0 copy-done.4
  135.1 1.0 copy-done.5
  136.1 15.3 %finish.1 = (f32[512,2048]{1,0:T(8,128)}, f32[1024,2048]{1,0:T(8,128)}) custom-call(s32[16]{0:T(128)S(1)} %stack.261.table_ref, f32[64,2048]{1,0:T(8,128)S(1)} %pad_maximum_fusion.1.refs_0_, f32[64,2048]{1,0:T(8,128)} %collective-permute-done.29.refs_1_, f32[64,2048]{1,0:T(8,128)S(1)} %pad_maximum_fusion.2.refs_2_, ...), custom_call_target="tpu_custom_call" | custom-call | tf_op jit(solution)/shard_map/finish/pallas_call | solution.py:294
  (104 shorter events, 5.9 us)
Async XLA Ops:
  1.5 7.7 %collective-permute-start.12 = (f32[64,128]{1,0:T(8,128)S(1)}, f32[64,128]{1,0:T(8,128)S(1)}, u32[]{:S(2)}, u32[]{:S(2)}) collective-permute-start(f32[64,128]{1,0:T(8,128)S(1)} %get-tuple-element.75), channel_id=1, source_target_pairs={{0,12},{1,13},{2,14},{3,15},{4,8},{5,9},{6,10},{7,11},{8,4},{9,5},... | collective-permute-start | bytes 98312 | tf_op jit(solution)/shard_map/ppermute | solution.py:169
  5.1 5.6 %collective-permute-start.4 = (f32[64,128]{1,0:T(8,128)S(1)}, f32[64,128]{1,0:T(8,128)S(1)}, u32[]{:S(2)}, u32[]{:S(2)}) collective-permute-start(f32[64,128]{1,0:T(8,128)S(1)} %get-tuple-element.80), channel_id=1, source_target_pairs={{0,3},{1,2},{2,1},{3,0},{4,7},{5,6},{6,5},{7,4},{8,11},{9,10},{10,... | collective-permute-start | bytes 98312 | tf_op jit(solution)/shard_map/ppermute | solution.py:169
  8.9 3.4 %collective-permute-start = (f32[64,128]{1,0:T(8,128)S(1)}, f32[64,128]{1,0:T(8,128)S(1)}, u32[]{:S(2)}, u32[]{:S(2)}) collective-permute-start(f32[64,128]{1,0:T(8,128)S(1)} %get-tuple-element.81), channel_id=1, source_target_pairs={{0,1},{1,0},{2,3},{3,2},{4,5},{5,4},{6,7},{7,6},{8,9},{9,8},{10,11... | collective-permute-start | bytes 98312 | tf_op jit(solution)/shard_map/ppermute | solution.py:169
  8.9 4.1 %collective-permute-start.8 = (f32[64,128]{1,0:T(8,128)S(1)}, f32[64,128]{1,0:T(8,128)S(1)}, u32[]{:S(2)}, u32[]{:S(2)}) collective-permute-start(f32[64,128]{1,0:T(8,128)S(1)} %get-tuple-element.82), channel_id=1, source_target_pairs={{0,4},{1,5},{2,6},{3,7},{4,0},{5,1},{6,2},{7,3},{8,12},{9,13},{10,... | collective-permute-start | bytes 98312 | tf_op jit(solution)/shard_map/ppermute | solution.py:169
  9.1 4.2 %collective-permute-start.13 = (f32[128,128]{1,0:T(8,128)S(1)}, f32[128,128]{1,0:T(8,128)S(1)}, u32[]{:S(2)}, u32[]{:S(2)}) collective-permute-start(f32[128,128]{1,0:T(8,128)S(1)} %pad_maximum_fusion.15), channel_id=1, source_target_pairs={{0,4},{1,5},{2,6},{3,7},{4,0},{5,1},{6,2},{7,3},{8,12},{9,13},{10,... | collective-permute-start | bytes 196616 | tf_op jit(solution)/shard_map/ppermute | solution.py:169
  10.7 4.6 %collective-permute-start.5 = (f32[128,128]{1,0:T(8,128)S(1)}, f32[128,128]{1,0:T(8,128)S(1)}, u32[]{:S(2)}, u32[]{:S(2)}) collective-permute-start(f32[128,128]{1,0:T(8,128)S(1)} %pad_maximum_fusion.13), channel_id=1, source_target_pairs={{0,1},{1,0},{2,3},{3,2},{4,5},{5,4},{6,7},{7,6},{8,9},{9,8},{10,11... | collective-permute-start | bytes 196616 | tf_op jit(solution)/shard_map/ppermute | solution.py:169
  12.2 5.8 %collective-permute-start.1 = (f32[128,128]{1,0:T(8,128)S(1)}, f32[128,128]{1,0:T(8,128)S(1)}, u32[]{:S(2)}, u32[]{:S(2)}) collective-permute-start(f32[128,128]{1,0:T(8,128)S(1)} %pad_maximum_fusion.12), channel_id=1, source_target_pairs={{0,3},{1,2},{2,1},{3,0},{4,7},{5,6},{6,5},{7,4},{8,11},{9,10},{10,... | collective-permute-start | bytes 196616 | tf_op jit(solution)/shard_map/ppermute | solution.py:169
  13.0 5.2 %collective-permute-start.9 = (f32[128,128]{1,0:T(8,128)S(1)}, f32[128,128]{1,0:T(8,128)S(1)}, u32[]{:S(2)}, u32[]{:S(2)}) collective-permute-start(f32[128,128]{1,0:T(8,128)S(1)} %pad_maximum_fusion.14), channel_id=1, source_target_pairs={{0,12},{1,13},{2,14},{3,15},{4,8},{5,9},{6,10},{7,11},{8,4},{9,5},... | collective-permute-start | bytes 196616 | tf_op jit(solution)/shard_map/ppermute | solution.py:169
  13.3 11.4 %collective-permute-start.14 = (f32[256,128]{1,0:T(8,128)S(1)}, f32[256,128]{1,0:T(8,128)S(1)}, u32[]{:S(2)}, u32[]{:S(2)}) collective-permute-start(f32[256,128]{1,0:T(8,128)S(1)} %pad_maximum_fusion.11), channel_id=1, source_target_pairs={{0,3},{1,2},{2,1},{3,0},{4,7},{5,6},{6,5},{7,4},{8,11},{9,10},{10,... | collective-permute-start | bytes 393224 | tf_op jit(solution)/shard_map/ppermute | solution.py:169
  15.3 8.8 %collective-permute-start.6 = (f32[256,128]{1,0:T(8,128)S(1)}, f32[256,128]{1,0:T(8,128)S(1)}, u32[]{:S(2)}, u32[]{:S(2)}) collective-permute-start(f32[256,128]{1,0:T(8,128)S(1)} %pad_maximum_fusion.9), channel_id=1, source_target_pairs={{0,12},{1,13},{2,14},{3,15},{4,8},{5,9},{6,10},{7,11},{8,4},{9,5},... | collective-permute-start | bytes 393224 | tf_op jit(solution)/shard_map/ppermute | solution.py:169
  18.0 6.0 %collective-permute-start.2 = (f32[256,128]{1,0:T(8,128)S(1)}, f32[256,128]{1,0:T(8,128)S(1)}, u32[]{:S(2)}, u32[]{:S(2)}) collective-permute-start(f32[256,128]{1,0:T(8,128)S(1)} %pad_maximum_fusion.8), channel_id=1, source_target_pairs={{0,4},{1,5},{2,6},{3,7},{4,0},{5,1},{6,2},{7,3},{8,12},{9,13},{10,... | collective-permute-start | bytes 393224 | tf_op jit(solution)/shard_map/ppermute | solution.py:169
  18.2 3.9 %collective-permute-start.10 = (f32[256,128]{1,0:T(8,128)S(1)}, f32[256,128]{1,0:T(8,128)S(1)}, u32[]{:S(2)}, u32[]{:S(2)}) collective-permute-start(f32[256,128]{1,0:T(8,128)S(1)} %pad_maximum_fusion.10), channel_id=1, source_target_pairs={{0,1},{1,0},{2,3},{3,2},{4,5},{5,4},{6,7},{7,6},{8,9},{9,8},{10,11... | collective-permute-start | bytes 393224 | tf_op jit(solution)/shard_map/ppermute | solution.py:169
  22.1 6.5 %collective-permute-start.11 = (f32[512,128]{1,0:T(8,128)S(1)}, f32[512,128]{1,0:T(8,128)S(1)}, u32[]{:S(2)}, u32[]{:S(2)}) collective-permute-start(f32[512,128]{1,0:T(8,128)S(1)} %pad_maximum_fusion.6), channel_id=1, source_target_pairs={{0,3},{1,2},{2,1},{3,0},{4,7},{5,6},{6,5},{7,4},{8,11},{9,10},{10,... | collective-permute-start | bytes 786440 | tf_op jit(solution)/shard_map/ppermute | solution.py:169
  24.0 6.5 %collective-permute-start.3 = (f32[512,128]{1,0:T(8,128)S(1)}, f32[512,128]{1,0:T(8,128)S(1)}, u32[]{:S(2)}, u32[]{:S(2)}) collective-permute-start(f32[512,128]{1,0:T(8,128)S(1)} %pad_maximum_fusion.4), channel_id=1, source_target_pairs={{0,12},{1,13},{2,14},{3,15},{4,8},{5,9},{6,10},{7,11},{8,4},{9,5},... | collective-permute-start | bytes 786440 | tf_op jit(solution)/shard_map/ppermute | solution.py:169
  24.2 11.3 %copy-start = (f32[1024,2048]{1,0:T(8,128)S(1)}, f32[1024,2048]{1,0:T(8,128)}, u32[]{:S(2)}) copy-start(f32[1024,2048]{1,0:T(8,128)} %refs_12_.1) | copy-start | bytes 25165828
  24.2 6.4 %collective-permute-start.7 = (f32[512,128]{1,0:T(8,128)S(1)}, f32[512,128]{1,0:T(8,128)S(1)}, u32[]{:S(2)}, u32[]{:S(2)}) collective-permute-start(f32[512,128]{1,0:T(8,128)S(1)} %pad_maximum_fusion.5), channel_id=1, source_target_pairs={{0,4},{1,5},{2,6},{3,7},{4,0},{5,1},{6,2},{7,3},{8,12},{9,13},{10,... | collective-permute-start | bytes 786440 | tf_op jit(solution)/shard_map/ppermute | solution.py:169
  24.8 5.8 %collective-permute-start.15 = (f32[512,128]{1,0:T(8,128)S(1)}, f32[512,128]{1,0:T(8,128)S(1)}, u32[]{:S(2)}, u32[]{:S(2)}) collective-permute-start(f32[512,128]{1,0:T(8,128)S(1)} %pad_maximum_fusion.7), channel_id=1, source_target_pairs={{0,1},{1,0},{2,3},{3,2},{4,5},{5,4},{6,7},{7,6},{8,9},{9,8},{10,11... | collective-permute-start | bytes 786440 | tf_op jit(solution)/shard_map/ppermute | solution.py:169
  34.7 6.6 %copy-start.2 = (f32[1024,512]{1,0:T(8,128)}, f32[1024,512]{1,0:T(8,128)S(1)}, u32[]{:S(2)}) copy-start(f32[1024,512]{1,0:T(8,128)S(1)} %get-tuple-element.32.p_ref) | copy-start | bytes 6291460
  41.3 35.5 %collective-permute-start.16 = (f32[256,2048]{1,0:T(8,128)}, f32[256,2048]{1,0:T(8,128)}, u32[]{:S(2)}, u32[]{:S(2)}) collective-permute-start(f32[256,2048]{1,0:T(8,128)} %share.3), channel_id=1, source_target_pairs={{0,16},{16,0},{32,48},{48,32},{64,80},{80,64},{96,112},{112,96},{1... | collective-permute-start | bytes 6291464 | tf_op jit(solution)/shard_map/ppermute | solution.py:194
  47.1 4.1 %collective-permute-start.19 = (f32[640,128]{1,0:T(8,128)S(1)}, f32[640,128]{1,0:T(8,128)S(1)}, u32[]{:S(2)}, u32[]{:S(2)}) collective-permute-start(f32[640,128]{1,0:T(8,128)S(1)} %get-tuple-element.36), channel_id=1, source_target_pairs={{0,16},{16,0},{32,48},{48,32},{64,80},{80,64},{96,112},{112,96},{1... | collective-permute-start | bytes 983048 | tf_op jit(solution)/shard_map/ppermute | solution.py:194
  51.3 5.7 %collective-permute-start.20 = (f32[320,128]{1,0:T(8,128)S(1)}, f32[320,128]{1,0:T(8,128)S(1)}, u32[]{:S(2)}, u32[]{:S(2)}) collective-permute-start(f32[320,128]{1,0:T(8,128)S(1)} %get-tuple-element.73), channel_id=1, source_target_pairs={{0,32},{16,48},{32,0},{48,16},{64,96},{80,112},{96,64},{112,80},{1... | collective-permute-start | bytes 491528 | tf_op jit(solution)/shard_map/ppermute | solution.py:194
  52.6 6.6 %collective-permute-start.22 = (f32[320,128]{1,0:T(8,128)S(1)}, f32[320,128]{1,0:T(8,128)S(1)}, u32[]{:S(2)}, u32[]{:S(2)}) collective-permute-start(f32[320,128]{1,0:T(8,128)S(1)} %get-tuple-element.74), channel_id=1, source_target_pairs={{0,96},{16,112},{32,64},{48,80},{64,32},{80,48},{96,0},{112,16},{1... | collective-permute-start | bytes 491528 | tf_op jit(solution)/shard_map/ppermute | solution.py:194
  59.1 5.5 %collective-permute-start.21 = (f32[320,128]{1,0:T(8,128)S(1)}, f32[320,128]{1,0:T(8,128)S(1)}, u32[]{:S(2)}, u32[]{:S(2)}) collective-permute-start(f32[320,128]{1,0:T(8,128)S(1)} %get-tuple-element.71), channel_id=1, source_target_pairs={{0,96},{16,112},{32,64},{48,80},{64,32},{80,48},{96,0},{112,16},{1... | collective-permute-start | bytes 491528 | tf_op jit(solution)/shard_map/ppermute | solution.py:194
  61.0 4.5 %collective-permute-start.23 = (f32[320,128]{1,0:T(8,128)S(1)}, f32[320,128]{1,0:T(8,128)S(1)}, u32[]{:S(2)}, u32[]{:S(2)}) collective-permute-start(f32[320,128]{1,0:T(8,128)S(1)} %get-tuple-element.72), channel_id=1, source_target_pairs={{0,32},{16,48},{32,0},{48,16},{64,96},{80,112},{96,64},{112,80},{1... | collective-permute-start | bytes 491528 | tf_op jit(solution)/shard_map/ppermute | solution.py:194
  65.6 11.1 %collective-permute-start.24 = (f32[640,128]{1,0:T(8,128)S(1)}, f32[640,128]{1,0:T(8,128)S(1)}, u32[]{:S(2)}, u32[]{:S(2)}) collective-permute-start(f32[640,128]{1,0:T(8,128)S(1)} %pad_maximum_fusion.3), channel_id=1, source_target_pairs={{0,16},{16,0},{32,48},{48,32},{64,80},{80,64},{96,112},{112,96},{1... | collective-permute-start | bytes 983048 | tf_op jit(solution)/shard_map/ppermute | solution.py:194
  68.1 3.4 %copy-start.1 = (f32[1024,2048]{1,0:T(8,128)S(1)}, f32[1024,2048]{1,0:T(8,128)}, u32[]{:S(2)}) copy-start(f32[1024,2048]{1,0:T(8,128)} %refs_12_.1) | copy-start | bytes 25165828
  78.6 14.8 %collective-permute-start.18 = (f32[64,2048]{1,0:T(8,128)S(1)}, f32[64,2048]{1,0:T(8,128)S(1)}, u32[]{:S(2)}, u32[]{:S(2)}) collective-permute-start(f32[64,2048]{1,0:T(8,128)S(1)} %get-tuple-element.62), channel_id=1, source_target_pairs={{0,96},{16,112},{32,64},{48,80},{64,32},{80,48},{96,0},{112,16},{1... | collective-permute-start | bytes 1572872 | tf_op jit(solution)/shard_map/ppermute | solution.py:194
  83.3 13.3 %collective-permute-start.17 = (f32[64,2048]{1,0:T(8,128)S(1)}, f32[64,2048]{1,0:T(8,128)S(1)}, u32[]{:S(2)}, u32[]{:S(2)}) collective-permute-start(f32[64,2048]{1,0:T(8,128)S(1)} %get-tuple-element.63), channel_id=1, source_target_pairs={{0,32},{16,48},{32,0},{48,16},{64,96},{80,112},{96,64},{112,80},{1... | collective-permute-start | bytes 1572872 | tf_op jit(solution)/shard_map/ppermute | solution.py:194
  87.5 19.0 %copy-start.6 = (f32[128,640]{1,0:T(8,128)}, f32[128,640]{1,0:T(8,128)S(1)}, u32[]{:S(2)}) copy-start(f32[128,640]{1,0:T(8,128)S(1)} %factor.5.refs_1_.w1) | copy-start | bytes 983044
  96.7 8.0 %collective-permute-start.25 = (f32[32,2048]{1,0:T(8,128)S(1)}, f32[32,2048]{1,0:T(8,128)S(1)}, u32[]{:S(2)}, u32[]{:S(2)}) collective-permute-start(f32[32,2048]{1,0:T(8,128)S(1)} %get-tuple-element.38), channel_id=1, source_target_pairs={{0,96},{16,112},{32,64},{48,80},{64,32},{80,48},{96,0},{112,16},{1... | collective-permute-start | bytes 786440 | tf_op jit(solution)/shard_map/ppermute | solution.py:194
  98.5 6.4 %collective-permute-start.26 = (f32[32,2048]{1,0:T(8,128)S(1)}, f32[32,2048]{1,0:T(8,128)S(1)}, u32[]{:S(2)}, u32[]{:S(2)}) collective-permute-start(f32[32,2048]{1,0:T(8,128)S(1)} %get-tuple-element.40), channel_id=1, source_target_pairs={{0,32},{16,48},{32,0},{48,16},{64,96},{80,112},{96,64},{112,80},{1... | collective-permute-start | bytes 786440 | tf_op jit(solution)/shard_map/ppermute | solution.py:194
  102.6 8.1 %copy-start.8 = (f32[128,640]{1,0:T(8,128)}, f32[128,640]{1,0:T(8,128)S(1)}, u32[]{:S(2)}) copy-start(f32[128,640]{1,0:T(8,128)S(1)} %factor.6.refs_2_.w2) | copy-start | bytes 983044
  104.9 6.5 %collective-permute-start.27 = (f32[32,2048]{1,0:T(8,128)S(1)}, f32[32,2048]{1,0:T(8,128)S(1)}, u32[]{:S(2)}, u32[]{:S(2)}) collective-permute-start(f32[32,2048]{1,0:T(8,128)S(1)} %add.293), channel_id=1, source_target_pairs={{0,96},{16,112},{32,64},{48,80},{64,32},{80,48},{96,0},{112,16},{1... | collective-permute-start | bytes 786440 | tf_op jit(solution)/shard_map/ppermute | solution.py:194
  106.5 5.5 %collective-permute-start.28 = (f32[32,2048]{1,0:T(8,128)S(1)}, f32[32,2048]{1,0:T(8,128)S(1)}, u32[]{:S(2)}, u32[]{:S(2)}) collective-permute-start(f32[32,2048]{1,0:T(8,128)S(1)} %add.294), channel_id=1, source_target_pairs={{0,32},{16,48},{32,0},{48,16},{64,96},{80,112},{96,64},{112,80},{1... | collective-permute-start | bytes 786440 | tf_op jit(solution)/shard_map/ppermute | solution.py:194
  110.8 15.9 %copy-start.10 = (f32[128,640]{1,0:T(8,128)}, f32[128,640]{1,0:T(8,128)S(1)}, u32[]{:S(2)}) copy-start(f32[128,640]{1,0:T(8,128)S(1)} %factor.7.w3) | copy-start | bytes 983044
  110.8 17.4 %copy-start.3 = (f32[1024,512]{1,0:T(8,128)S(1)}, f32[1024,512]{1,0:T(8,128)}, u32[]{:S(2)}) copy-start(f32[1024,512]{1,0:T(8,128)} %copy-done.2) | copy-start | bytes 6291460
  112.1 10.4 %collective-permute-start.29 = (f32[64,2048]{1,0:T(8,128)S(1)}, f32[64,2048]{1,0:T(8,128)}, u32[]{:S(2)}, u32[]{:S(2)}) collective-permute-start(f32[64,2048]{1,0:T(8,128)S(1)} %pad_maximum_fusion.1.refs_0_), channel_id=1, source_target_pairs={{0,32},{16,48},{32,0},{48,16},{64,96},{80,112},{96,64},{112,80},{1... | collective-permute-start | bytes 1572872 | tf_op jit(solution)/shard_map/ppermute | solution.py:194
  112.4 14.2 %collective-permute-start.30 = (f32[64,2048]{1,0:T(8,128)S(1)}, f32[64,2048]{1,0:T(8,128)}, u32[]{:S(2)}, u32[]{:S(2)}) collective-permute-start(f32[64,2048]{1,0:T(8,128)S(1)} %pad_maximum_fusion.2.refs_2_), channel_id=1, source_target_pairs={{0,96},{16,112},{32,64},{48,80},{64,32},{80,48},{96,0},{112,16},{1... | collective-permute-start | bytes 1572872 | tf_op jit(solution)/shard_map/ppermute | solution.py:194
  113.7 22.4 %collective-permute-start.31 = (f32[64,2048]{1,0:T(8,128)S(1)}, f32[64,2048]{1,0:T(8,128)}, u32[]{:S(2)}, u32[]{:S(2)}) collective-permute-start(f32[64,2048]{1,0:T(8,128)S(1)} %pad_maximum_fusion.1.refs_0_), channel_id=1, source_target_pairs={{0,16},{16,0},{32,48},{48,32},{64,80},{80,64},{96,112},{112,96},{1... | collective-permute-start | bytes 1572872 | tf_op jit(solution)/shard_map/ppermute | solution.py:194
  117.1 19.0 %collective-permute-start.33 = (f32[64,2048]{1,0:T(8,128)S(1)}, f32[64,2048]{1,0:T(8,128)}, u32[]{:S(2)}, u32[]{:S(2)}) collective-permute-start(f32[64,2048]{1,0:T(8,128)S(1)} %pad_maximum_fusion.2.refs_2_), channel_id=1, source_target_pairs={{0,16},{16,0},{32,48},{48,32},{64,80},{80,64},{96,112},{112,96},{1... | collective-permute-start | bytes 1572872 | tf_op jit(solution)/shard_map/ppermute | solution.py:194
  122.5 13.6 %collective-permute-start.32 = (f32[64,2048]{1,0:T(8,128)}, f32[64,2048]{1,0:T(8,128)}, u32[]{:S(2)}, u32[]{:S(2)}) collective-permute-start(f32[64,2048]{1,0:T(8,128)} %collective-permute-done.29.refs_1_), channel_id=1, source_target_pairs={{0,16},{16,0},{32,48},{48,32},{64,80},{80,64},{96,112},{112,96},{1... | collective-permute-start | bytes 1572872 | tf_op jit(solution)/shard_map/ppermute | solution.py:194
  126.6 9.5 %collective-permute-start.34 = (f32[64,2048]{1,0:T(8,128)}, f32[64,2048]{1,0:T(8,128)}, u32[]{:S(2)}, u32[]{:S(2)}) collective-permute-start(f32[64,2048]{1,0:T(8,128)} %collective-permute-done.30.refs_3_), channel_id=1, source_target_pairs={{0,16},{16,0},{32,48},{48,32},{64,80},{80,64},{96,112},{112,96},{1... | collective-permute-start | bytes 1572872 | tf_op jit(solution)/shard_map/ppermute | solution.py:194
  128.2 1.0 copy-start.7
  129.2 1.0 copy-start.9
  130.1 1.0 copy-start.11
  134.1 1.0 copy-start.4
  135.1 1.0 copy-start.5
where the time goes:
time: 152 us; the launch traced here: 151 us
  Pallas kernels  50 us (33%)
  starting transfers between devices  47.6 us (31%)
  waiting for transfers between devices  40.4 us (27%)
  local copies, waits for them, and re-layouts  9.73 us (6%)
  other arithmetic  2.49 us (2%)
    ppermute x19, waiting for transfers between devices, swap(): return lax.ppermute(a, 'row', pairs)  31.1 us
    ppermute x19, starting transfers between devices, swap(): return lax.ppermute(a, 'row', pairs)  28.5 us
    ppermute x16, starting transfers between devices, gather_panel(): got.append(lax.ppermute(held[q], 'col', pairs[axis][side]))  19.1 us
    pallas_call x4, Pallas kernels, factor_rows(): pl.pallas_call(functools.partial(factor_kernel, k, nb), out_shape=jax.Sha...  16 us
    pallas_call x1, Pallas kernels, finish(): pl.pallas_call(finish_kernel, out_shape=(jax.ShapeDtypeStruct((b, width),...  15.3 us
    pallas_call x2, Pallas kernels, share(): pl.pallas_call(share_kernel, out_shape=jax.ShapeDtypeStruct((256, width),...  10.9 us
    ppermute x16, waiting for transfers between devices, gather_panel(): got.append(lax.ppermute(held[q], 'col', pairs[axis][side]))  9.3 us
    unnamed x36, local copies, waits for them, and re-layouts  8.39 us
  transfers between devices with their start and end apart: 35, of which 15 were waited for; matrix products, arithmetic and copies ran while one was open for 1% of the time, Pallas kernels for 16%

commit v1 on v0

--- a/solution.py
+++ b/solution.py
@@ -12,6 +12,7 @@
 F32 = jnp.float32
 GROUP = 32
 TILE = 512
+NARROW = 256
 
 
 def near(i):
@@ -24,8 +25,6 @@
 
 CORE = [(r, r ^ 1) for r in range(8)]
 XPAIR = [[(x * 2 + c, pair(x) * 2 + c) for x in range(4) for c in range(2)] for pair in (near, far)]
-YPAIR = [[(y * 4 + z, pair(y) * 4 + z) for y in range(4) for z in range(4)] for pair in (near, far)]
-ZPAIR = [[(y * 4 + z, y * 4 + pair(z)) for y in range(4) for z in range(4)] for pair in (near, far)]
 
 
 def ring_bits(i):
@@ -76,6 +75,10 @@
     return pltpu.CompilerParams(vmem_limit_bytes=mib << 20)
 
 
+def cheap():
+    return pl.CostEstimate(flops=3 * 10 ** 8, bytes_accessed=10 ** 6, transcendentals=0)
+
+
 def whole(n=1):
     return [pl.BlockSpec(memory_space=pltpu.VMEM)] * n
 
@@ -128,61 +131,89 @@
         out_specs=whole()[0],
         scratch_shapes=[pltpu.VMEM((128, window), F32)],
         compiler_params=params(16),
-        cost_estimate=pl.CostEstimate(flops=5 * 10 ** 9, bytes_accessed=18 * 10 ** 6, transcendentals=0),
+        cost_estimate=cheap(),
         name="factor",
     )(*earlier, packed)
 
 
-def gram_kernel(order_ref, a0, a1, a2, a3, o_ref, keep_ref, give_ref, blocks):
-    for q, ref in enumerate((a0, a1, a2, a3)):
-        for p in range(16):
-            at = pl.multiple_of(order_ref[q * 16 + p] * 64, 64)
-            o_ref[pl.ds(at, 64), q * 128:q * 128 + 128] = ref[p * 64:p * 64 + 64, :]
+def shifts(axis):
+    out = []
+    for by in (1, 3, 2):
+        if axis == "y":
+            out.append((by, [(y * 4 + z, (y + by) % 4 * 4 + z) for y in range(4) for z in range(4)]))
+        else:
+            out.append((by, [(y * 4 + z, y * 4 + (z + by) % 4) for y in range(4) for z in range(4)]))
+    return out
+
+
+def gather_panel(panel):
+    col = lax.axis_index("col")
+    n = panel.shape[1] // 2
+    held = [panel[:, :n], panel[:, n:]]
+    place = [[(col // 4, col % 4)], [(col // 4, col % 4)]]
+    pieces = [None, None]
+    for step in (0, 1):
+        for q in (0, 1):
+            axis = "zy"[step ^ q]
+            pieces[q] = [held[q]]
+            known = list(place[q])
+            for by, pairs in shifts(axis):
+                pieces[q].append(lax.ppermute(held[q], "col", pairs))
+                place[q] += [((y - by) % 4, z) if axis == "y" else (y, (z - by) % 4) for y, z in known]
+        if step == 0:
+            held = [jnp.concatenate(p, axis=0) for p in pieces]
+    return pieces[0] + pieces[1], [y * 4 + z for q in (0, 1) for y, z in place[q]]
+
+
+def turn_kernel(order_ref, *refs):
+    pieces, (o_ref, hi_ref, lo_ref) = refs[:8], refs[8:]
+    for i, ref in enumerate(pieces):
+        q, four = divmod(i, 4)
+        for p in range(4):
+            at = pl.multiple_of(order_ref[i * 4 + p] * 64, 64)
+            o_ref[pl.ds(at, 64), q * 256:q * 256 + 256] = ref[p * 64:p * 64 + 64, :]
+    for j in range(0, 1024, 128):
+        hi_ref[:, j:j + 128], lo_ref[:, j:j + 128] = split(jnp.transpose(o_ref[j:j + 128, :]))
+
+
+def turn(pieces, order):
+    depth, b = pieces[0].shape[0] * 4, pieces[0].shape[1] * 2
+    out = jax.ShapeDtypeStruct((b, depth), BF16)
+    return pl.pallas_call(
+        turn_kernel,
+        out_shape=(jax.ShapeDtypeStruct((depth, b), F32), out, out),
+        in_specs=[SCALARS] + whole(8),
+        out_specs=whole(3),
+        compiler_params=params(),
+        cost_estimate=cheap(),
+        name="turn",
+    )(jnp.stack(order).astype(jnp.int32), *pieces)
+
+
+def gram_kernel(core_ref, p_ref, keep_ref, give_ref, blocks):
     at = 0
     for i in range(4):
-        strip = tdot(o_ref[:, i * 128:i * 128 + 128], o_ref[:, i * 128:])
+        strip = tdot(p_ref[:, i * 128:i * 128 + 128], p_ref[:, i * 128:])
         for j in range(4 - i):
             blocks[at:at + 128, :] = strip[:, j * 128:j * 128 + 128]
             at += 128
-    core = order_ref[64]
+    core = core_ref[0]
     keep_ref[...] = blocks[pl.ds(pl.multiple_of(core * 640, 128), 640), :]
     give_ref[...] = blocks[pl.ds(pl.multiple_of((1 - core) * 640, 128), 640), :]
 
 
-def gather_panel(panel, core):
-    col = lax.axis_index("col")
-    y, z = col // 4, col % 4
-    pairs = {"y": YPAIR, "z": ZPAIR}
-    orders = (
-        (("z", 0), ("z", 1), ("y", 0), ("y", 1)),
-        (("z", 1), ("z", 0), ("y", 1), ("y", 0)),
-        (("y", 0), ("y", 1), ("z", 0), ("z", 1)),
-        (("y", 1), ("y", 0), ("z", 1), ("z", 0)),
-    )
-    held = [panel[:, q * 128:q * 128 + 128] for q in range(4)]
-    where = [[(y, z)] for _ in range(4)]
-    flip = (near, far)
-    for step in range(4):
-        got = []
-        for q in range(4):
-            axis, side = orders[q][step]
-            got.append(lax.ppermute(held[q], "col", pairs[axis][side]))
-        for q in range(4):
-            axis, side = orders[q][step]
-            held[q] = jnp.concatenate([held[q], got[q]], axis=0)
-            other = [(flip[side](a), b) if axis == "y" else (a, flip[side](b)) for a, b in where[q]]
-            where[q] = where[q] + other
-    table = jnp.stack([a * 4 + b for q in range(4) for a, b in where[q]] + [core]).astype(jnp.int32)
+def gram_share(rows, core):
     half = jax.ShapeDtypeStruct((640, 128), F32)
     return pl.pallas_call(
         gram_kernel,
-        out_shape=(jax.ShapeDtypeStruct((1024, 512), F32), half, half),
-        in_specs=[SCALARS] + whole(4),
-        out_specs=whole(3),
+        out_shape=(half, half),
+        in_specs=[SCALARS] + whole(),
+        out_specs=whole(2),
         scratch_shapes=[pltpu.VMEM((1280, 128), F32)],
         compiler_params=params(),
+        cost_estimate=cheap(),
         name="gram",
-    )(table, *held)
+    )(core.reshape(1).astype(jnp.int32), rows)
 
 
 def join(own, other, bit):
@@ -194,48 +225,50 @@
     return lax.ppermute(a, "row", pairs)
 
 
-def sum_packed(keep, give, core):
-    a = keep + swap(give, CORE)
-    n = a.shape[0] // 2
-    one, two = a[:n], a[n:]
-    for side in (0, 1):
-        one, two = one + swap(one, XPAIR[side]), two + swap(two, XPAIR[1 - side])
-    a = jnp.concatenate([one, two], axis=0)
-    return join(a, swap(a, CORE), core)
-
-
-def turn_kernel(p_ref, hi_ref, lo_ref):
-    for j in range(0, 1024, 128):
-        hi_ref[:, j:j + 128], lo_ref[:, j:j + 128] = split(jnp.transpose(p_ref[j:j + 128, :]))
-
-
-def turn(rows):
-    out = jax.ShapeDtypeStruct((rows.shape[1], rows.shape[0]), BF16)
-    return pl.pallas_call(
-        turn_kernel, out_shape=(out, out), in_specs=whole(), out_specs=whole(2), compiler_params=params(), name="turn"
-    )(rows)
-
-
-def share_kernel(table_ref, hi_ref, lo_ref, t_ref, o_ref):
-    rows = pl.ds(pl.multiple_of(table_ref[0] * 256, 256), 256)
-    got = dot3((hi_ref[rows, :], lo_ref[rows, :]), split(t_ref[...]))
-    for p in range(8):
-        at = pl.multiple_of(table_ref[1 + p] * 32, 32)
-        o_ref[pl.ds(at, 32), :] = got[p * 32:p * 32 + 32, :]
-
-
-def share(table, hi, lo, trailing):
-    depth, width = trailing.shape
+def share_kernel(table_ref, hi_ref, lo_ref, t_ref, keep_ref, give_ref, total):
+    got = dot3((hi_ref[...], lo_ref[...]), split(t_ref[...]))
+    for p in range(16):
+        at = pl.multiple_of(table_ref[p] * 32, 32)
+        total[pl.ds(at, 32), :] = got[p * 32:p * 32 + 32, :]
+    keep_ref[...] = total[:256, :]
+    give_ref[...] = total[256:, :]
+
+
+def share(table, hi, lo, trailing, first, width):
+    depth = trailing.shape[0]
+    half = jax.ShapeDtypeStruct((256, width), F32)
+    out = pl.BlockSpec((256, TILE), lambda i: (0, i))
     return pl.pallas_call(
         share_kernel,
-        out_shape=jax.ShapeDtypeStruct((256, width), F32),
+        out_shape=(half, half),
         grid=(width // TILE,),
-        in_specs=[SCALARS] + whole(2) + [pl.BlockSpec((depth, TILE), lambda i: (0, i))],
-        out_specs=pl.BlockSpec((256, TILE), lambda i: (0, i)),
+        in_specs=[SCALARS] + whole(2) + [pl.BlockSpec((depth, TILE), lambda i: (0, i + first // TILE))],
+        out_specs=(out, out),
+        scratch_shapes=[pltpu.VMEM((512, TILE), F32)],
         compiler_params=params(),
-        cost_estimate=pl.CostEstimate(flops=3 * 10 ** 9, bytes_accessed=12 * 10 ** 6, transcendentals=0),
+        cost_estimate=cheap(),
         name="share",
     )(table, hi, lo, trailing)
+
+
+def fold_kernel(k0, k1, g0, g1, a_give, b_give, a_keep, b_keep):
+    n = k0.shape[1]
+    for cols, k, g in ((slice(0, n), k0, g0), (slice(n, 2 * n), k1, g1)):
+        for at, ref in ((64, a_give), (192, b_give), (0, a_keep), (128, b_keep)):
+            ref[:, cols] = k[at:at + 64, :] + g[at:at + 64, :]
+
+
+def fold(keeps, gots):
+    out = jax.ShapeDtypeStruct((64, 2 * keeps[0].shape[1]), F32)
+    return pl.pallas_call(
+        fold_kernel,
+        out_shape=(out,) * 4,
+        in_specs=whole(4),
+        out_specs=whole(4),
+        compiler_params=params(),
+        cost_estimate=cheap(),
+        name="fold",
+    )(*keeps, *gots)
 
 
 def prepare_kernel(w0, w1, w2, w3, p_ref, r_ref, ihi_ref, ilo_ref, bhi_ref, blo_ref, inv):
@@ -269,7 +302,7 @@
         out_specs=whole(5),
         scratch_shapes=[pltpu.VMEM(square, F32)],
         compiler_params=params(),
-        cost_estimate=pl.CostEstimate(flops=3 * 10 ** 9, bytes_accessed=10 * 10 ** 6, transcendentals=0),
+        cost_estimate=cheap(),
         name="prepare",
     )(*factors, rows)
 
@@ -294,55 +327,67 @@
     return pl.pallas_call(
         finish_kernel,
         out_shape=(jax.ShapeDtypeStruct((b, width), F32), jax.ShapeDtypeStruct((depth, width), F32)),
-        grid=(width // TILE,),
+        grid=(width // NARROW,),
         in_specs=[SCALARS]
-        + [pl.BlockSpec((64, TILE), lambda i: (0, i))] * 8
+        + [pl.BlockSpec((64, NARROW), lambda i: (0, i))] * 8
         + whole(4)
-        + [pl.BlockSpec((depth, TILE), lambda i: (0, i))],
-        out_specs=(pl.BlockSpec((b, TILE), lambda i: (0, i)), pl.BlockSpec((depth, TILE), lambda i: (0, i))),
-        scratch_shapes=[pltpu.VMEM((b, TILE), F32)],
+        + [pl.BlockSpec((depth, NARROW), lambda i: (0, i))],
+        out_specs=(pl.BlockSpec((b, NARROW), lambda i: (0, i)), pl.BlockSpec((depth, NARROW), lambda i: (0, i))),
+        scratch_shapes=[pltpu.VMEM((b, NARROW), F32)],
         compiler_params=params(48),
         name="finish",
     )(table, *pieces, ihi, ilo, bhi, blo, trailing)
+
+
+def after(value, *others):
+    return lax.optimization_barrier((value, others))[0]
 
 
 def local(panel, trailing):
     row = lax.axis_index("row")
     core = row % 2
     bits = ring_bits(row // 2)
-    rows, keep, give = gather_panel(panel, core)
-    packed = sum_packed(keep, give, core)
-    hi, lo = turn(rows)
-
-    def held(part, i, j):
+    pieces, order = gather_panel(panel)
+    rows, hi, lo = turn(pieces, order)
+
+    def held(half, part, i, j):
         s, t = (bits[0], bits[1]) if part == 0 else (bits[1], bits[0])
-        return part * 4 + (i ^ s) * 2 + (j ^ t)
-
-    spots = [held(part, i, j) for part in (0, 1) for i in (0, 1) for j in (0, 1)]
-    give = share(jnp.stack([1 - core] + spots).astype(jnp.int32), hi, lo, trailing)
-    keep = share(jnp.stack([core] + spots).astype(jnp.int32), hi, lo, trailing)
-    got = swap(give, CORE)
-    parts = [[keep[at:at + 64] + got[at:at + 64], keep[at + 64:at + 128] + got[at + 64:at + 128]] for at in (0, 128)]
-    came = [swap(parts[h][1], XPAIR[h]) for h in (0, 1)]
-    parts = [[parts[h][0][:32] + came[h][:32], parts[h][0][32:] + came[h][32:]] for h in (0, 1)]
-
+        return (half ^ core) * 8 + part * 4 + (i ^ s) * 2 + (j ^ t)
+
+    spots = [held(half, part, i, j) for half in (0, 1) for part in (0, 1) for i in (0, 1) for j in (0, 1)]
+    table = jnp.stack(spots).astype(jnp.int32)
+    width = trailing.shape[1] // 2
+    keep, give = zip(*[share(table, hi, lo, trailing, at, width) for at in (0, width)])
+    got = [swap(g, CORE) for g in give]
+    a_give, b_give, a_keep, b_keep = fold(keep, got)
+
+    came = [swap(g, XPAIR[h]) for h, g in ((0, a_give), (1, b_give))]
+    gram_keep, gram_give = gram_share(after(rows, a_give), core)
+    gram = gram_keep + swap(gram_give, CORE)
+    n = gram.shape[0] // 2
+    one, two = gram[:n], gram[n:]
+    one, two = one + swap(one, XPAIR[0]), two + swap(two, XPAIR[1])
+
+    parts = [(k[:32] + c[:32], k[32:] + c[32:]) for k, c in zip((a_keep, b_keep), came)]
+    came = [swap(parts[h][1], XPAIR[1 - h]) for h in (0, 1)]
+    one, two = one + swap(one, XPAIR[1]), two + swap(two, XPAIR[0])
+    gram = jnp.concatenate([one, two], axis=0)
+    packed = join(gram, swap(gram, CORE), core)
+
+    own = [parts[h][0] + came[h] for h in (0, 1)]
+    came = [swap(own[h], XPAIR[1 - h]) for h in (0, 1)]
     factors = [factor_rows(0, 4, [], packed)]
     factors.append(factor_rows(1, 4, factors, packed))
-    parts, factors = lax.optimization_barrier((parts, factors))
-    came = [swap(parts[h][1], XPAIR[1 - h]) for h in (0, 1)]
-    own = [parts[h][0] + came[h] for h in (0, 1)]
-    factors.append(factor_rows(2, 4, factors, packed))
-    own, factors = lax.optimization_barrier((own, factors))
-    came = [swap(own[h], XPAIR[1 - h]) for h in (0, 1)]
     own = [jnp.concatenate([own[h], came[h]], axis=0) for h in (0, 1)]
-    factors.append(factor_rows(3, 4, factors, packed))
     own, factors = lax.optimization_barrier((own, factors))
     came = [swap(own[h], XPAIR[h]) for h in (0, 1)]
+    factors.append(factor_rows(2, 4, factors, packed))
+    factors.append(factor_rows(3, 4, factors, packed))
     r_factor, ihi, ilo, bhi, blo = prepare(factors, rows)
+    came, ihi = lax.optimization_barrier((came, ihi))
     mine = [own[0], came[0], own[1], came[1]]
     theirs = [swap(p, CORE) for p in mine]
-    spots = [c * 8 + s for c in (core, 1 - core) for s in spots]
-    coupling, out = finish(jnp.stack(spots).astype(jnp.int32), mine + theirs, ihi, ilo, bhi, blo, trailing)
+    coupling, out = finish(table, mine + theirs, ihi, ilo, bhi, blo, trailing)
     return (r_factor, coupling, out)
 
 

time: 152 us -> 152 us (level)
  Pallas kernels: 50 us -> 55.8 us
  waiting for transfers between devices: 40.4 us -> 34.9 us
  starting transfers between devices: 47.6 us -> 44.4 us
  local copies, waits for them, and re-layouts: 9.73 us -> 12.2 us
    ppermute x19 -> x20, waiting for transfers between devices: 31.1 us -> 21.9 us  [swap(): return lax.ppermute(a, 'row', pairs)]
    pallas_call x1, Pallas kernels: 15.3 us -> 22 us  [finish(): pl.pallas_call(finish_kernel, out_shape=(jax.ShapeDtypeStruct((b, width),...]
    ppermute x16 -> x12, waiting for transfers between devices: 9.3 us -> 13.1 us  [gather_panel(): pieces[q].append(lax.ppermute(held[q], 'col', pairs))]
    ppermute x19 -> x20, starting transfers between devices: 28.5 us -> 25.8 us  [swap(): return lax.ppermute(a, 'row', pairs)]
    unnamed x36 -> x22, local copies, waits for them, and re-layouts: 8.39 us -> 10.3 us
    pallas_call x4 -> x5, Pallas kernels: 15.7 us -> 14.8 us  [the longest x2 9.28 us: share(): pl.pallas_call(share_kernel, out_shape=(half, half), grid=(width // TILE,...]
    ppermute x16 -> x12, starting transfers between devices: 19.1 us -> 18.6 us  [gather_panel(): pieces[q].append(lax.ppermute(held[q], 'col', pairs))]
  transfers between devices with their start and end apart: 35 -> 32, of which waited for: 15 -> 18; matrix products, arithmetic and copies ran while one was open for 1% -> 3% of each run, Pallas kernels for 16% -> 13%
where the time goes in v1:
time: 152 us
  Pallas kernels  55.8 us (37%)
  starting transfers between devices  44.4 us (29%)
  waiting for transfers between devices  34.9 us (23%)
  local copies, waits for them, and re-layouts  12.2 us (8%)
  other arithmetic  3.59 us (2%)
    ppermute x20, starting transfers between devices, swap(): return lax.ppermute(a, 'row', pairs)  25.8 us
    pallas_call x1, Pallas kernels, finish(): pl.pallas_call(finish_kernel, out_shape=(jax.ShapeDtypeStruct((b, width),...  22 us
    ppermute x20, waiting for transfers between devices, swap(): return lax.ppermute(a, 'row', pairs)  21.9 us
    ppermute x12, starting transfers between devices, gather_panel(): pieces[q].append(lax.ppermute(held[q], 'col', pairs))  18.6 us
    pallas_call x4, Pallas kernels, factor_rows(): pl.pallas_call(functools.partial(factor_kernel, k, nb), out_shape=jax.Sha...  16 us
    ppermute x12, waiting for transfers between devices, gather_panel(): pieces[q].append(lax.ppermute(held[q], 'col', pairs))  13.1 us
    unnamed x22, local copies, waits for them, and re-layouts  10.3 us
    pallas_call x2, Pallas kernels, share(): pl.pallas_call(share_kernel, out_shape=(half, half), grid=(width // TILE,...  9.28 us
  transfers between devices with their start and end apart: 32, of which 18 were waited for; matrix products, arithmetic and copies ran while one was open for 3% of the time, Pallas kernels for 13%

profile of v1, /device:TPU:1, one launch (start us, length us, event | category | flops | bytes accessed | tf_op | source)
XLA Modules:
  0.0 151.7 jit_solution(13764671701187851112)
XLA Ops:
  1.5 4.5 %collective-permute-start.2 = (f32[64,256]{1,0:T(8,128)S(1)}, f32[64,256]{1,0:T(8,128)S(1)}, u32[]{:S(2)}, u32[]{:S(2)}) collective-permute-start(f32[64,256]{1,0:T(8,128)S(1)} %get-tuple-element.66), channel_id=1, source_target_pairs={{0,2},{1,3},{2,0},{3,1},{4,6},{5,7},{6,4},{7,5},{8,10},{9,11},{10,... | collective-permute-start | bytes 196616 | tf_op jit(solution)/shard_map/ppermute | solution.py:161
  6.5 1.0 collective-permute-start
  7.7 1.8 %collective-permute-done.1 = f32[64,256]{1,0:T(8,128)S(1)} collective-permute-done((f32[64,256]{1,0:T(8,128)S(1)}, f32[64,256]{1,0:T(8,128)S(1)}, u32[]{:S(2)}, u32[]{:S(2)}) %collective-permute-start.1) | collective-permute-done | bytes 65568 | tf_op jit(solution)/shard_map/ppermute | solution.py:161
  9.5 1.3 collective-permute-done
  10.8 3.0 %collective-permute-start.5 = (f32[256,256]{1,0:T(8,128)S(1)}, f32[256,256]{1,0:T(8,128)S(1)}, u32[]{:S(2)}, u32[]{:S(2)}) collective-permute-start(f32[256,256]{1,0:T(8,128)S(1)} %pad_maximum_fusion.4.refs_0_), channel_id=1, source_target_pairs={{0,8},{1,9},{2,10},{3,11},{4,12},{5,13},{6,14},{7,15},{8,0},{9,1},... | collective-permute-start | bytes 786440 | tf_op jit(solution)/shard_map/ppermute | solution.py:161
  13.9 2.7 %collective-permute-start.7 = (f32[64,256]{1,0:T(8,128)S(1)}, f32[64,256]{1,0:T(8,128)S(1)}, u32[]{:S(2)}, u32[]{:S(2)}) collective-permute-start(f32[64,256]{1,0:T(8,128)S(1)} %get-tuple-element.65), channel_id=1, source_target_pairs={{0,12},{1,13},{2,14},{3,15},{4,0},{5,1},{6,2},{7,3},{8,4},{9,5},{1... | collective-permute-start | bytes 196616 | tf_op jit(solution)/shard_map/ppermute | solution.py:161
  16.6 2.7 %collective-permute-start.4 = (f32[256,256]{1,0:T(8,128)S(1)}, f32[256,256]{1,0:T(8,128)S(1)}, u32[]{:S(2)}, u32[]{:S(2)}) collective-permute-start(f32[256,256]{1,0:T(8,128)S(1)} %pad_maximum_fusion.4.refs_0_), channel_id=1, source_target_pairs={{0,12},{1,13},{2,14},{3,15},{4,0},{5,1},{6,2},{7,3},{8,4},{9,5},{1... | collective-permute-start | bytes 786440 | tf_op jit(solution)/shard_map/ppermute | solution.py:161
  19.4 1.1 collective-permute-start.3
  21.0 2.1 %collective-permute-done.6 = f32[64,256]{1,0:T(8,128)S(1)} collective-permute-done((f32[64,256]{1,0:T(8,128)S(1)}, f32[64,256]{1,0:T(8,128)S(1)}, u32[]{:S(2)}, u32[]{:S(2)}) %collective-permute-start.6) | collective-permute-done | bytes 65568 | tf_op jit(solution)/shard_map/ppermute | solution.py:161
  23.1 1.6 %collective-permute-start.11 = (f32[256,256]{1,0:T(8,128)S(1)}, f32[256,256]{1,0:T(8,128)S(1)}, u32[]{:S(2)}, u32[]{:S(2)}) collective-permute-start(f32[256,256]{1,0:T(8,128)S(1)} %pad_maximum_fusion.5.refs_4_), channel_id=1, source_target_pairs={{0,2},{1,3},{2,0},{3,1},{4,6},{5,7},{6,4},{7,5},{8,10},{9,11},{10,... | collective-permute-start | bytes 786440 | tf_op jit(solution)/shard_map/ppermute | solution.py:161
  24.6 1.2 collective-permute-start.10
  27.2 2.7 %collective-permute-done.11.refs_7_ = f32[256,256]{1,0:T(8,128)S(1)} collective-permute-done((f32[256,256]{1,0:T(8,128)S(1)}, f32[256,256]{1,0:T(8,128)S(1)}, u32[]{:S(2)}, u32[]{:S(2)}) %collective-permute-start.11) | collective-permute-done | bytes 262176 | tf_op jit(solution)/shard_map/ppermute | solution.py:161
  30.6 3.5 %collective-permute-done.10.refs_6_ = f32[256,256]{1,0:T(8,128)S(1)} collective-permute-done((f32[256,256]{1,0:T(8,128)S(1)}, f32[256,256]{1,0:T(8,128)S(1)}, u32[]{:S(2)}, u32[]{:S(2)}) %collective-permute-start.10) | collective-permute-done | bytes 262176 | tf_op jit(solution)/shard_map/ppermute | solution.py:161
  35.5 0.9 copy-done.4
  36.5 0.9 copy-done.6
  37.5 0.9 copy-done.8
  38.4 1.5 turn.1
  39.9 3.4 %copy-done = f32[1024,2048]{1,0:T(8,128)S(1)} copy-done((f32[1024,2048]{1,0:T(8,128)S(1)}, f32[1024,2048]{1,0:T(8,128)}, u32[]{:S(2)}) %copy-start) | copy-done | bytes 8388632
  43.2 4.6 %share.3 = (f32[256,1024]{1,0:T(8,128)S(1)}, f32[256,1024]{1,0:T(8,128)S(1)}) custom-call(s32[16]{0:T(128)S(1)} %stack.134.table_ref, bf16[512,1024]{1,0:T(8,128)(2,1)S(1)} %get-tuple-element.31.hi_ref, bf16[512,1024]{1,0:T(8,128)(2,1)S(1)} %get-tuple-element.32.lo_ref, f32[1024,2048]{1,0:T(8,128)S(1)} %copy-done), custom_call_target="tpu_custom_call" | custom-call | flops 300000000 | bytes 1000000 | tf_op jit(solution)/shard_map/share/pallas_call | solution.py:241
  47.9 4.6 %share.2 = (f32[256,1024]{1,0:T(8,128)S(1)}, f32[256,1024]{1,0:T(8,128)S(1)}) custom-call(s32[16]{0:T(128)S(1)} %stack.134.table_ref, bf16[512,1024]{1,0:T(8,128)(2,1)S(1)} %get-tuple-element.31.hi_ref, bf16[512,1024]{1,0:T(8,128)(2,1)S(1)} %get-tuple-element.32.lo_ref, f32[1024,2048]{1,0:T(8,128)S(1)} %copy-done), custom_call_target="tpu_custom_call" | custom-call | flops 300000000 | bytes 1000000 | tf_op jit(solution)/shard_map/share/pallas_call | solution.py:241
  52.5 4.2 %collective-permute-start.12 = (f32[256,1024]{1,0:T(8,128)S(1)}, f32[256,1024]{1,0:T(8,128)S(1)}, u32[]{:S(2)}, u32[]{:S(2)}) collective-permute-start(f32[256,1024]{1,0:T(8,128)S(1)} %get-tuple-element.35), channel_id=1, source_target_pairs={{0,16},{16,0},{32,48},{48,32},{64,80},{80,64},{96,112},{112,96},{1... | collective-permute-start | bytes 3145736 | tf_op jit(solution)/shard_map/ppermute | solution.py:225
  57.0 2.0 %collective-permute-done.12.g0 = f32[256,1024]{1,0:T(8,128)S(1)} collective-permute-done((f32[256,1024]{1,0:T(8,128)S(1)}, f32[256,1024]{1,0:T(8,128)S(1)}, u32[]{:S(2)}, u32[]{:S(2)}) %collective-permute-start.12) | collective-permute-done | bytes 1048608 | tf_op jit(solution)/shard_map/ppermute | solution.py:225
  59.1 1.5 collective-permute-done.13.g1
  60.6 1.0 fold.1
  61.6 3.1 %gram.1 = (f32[640,128]{1,0:T(8,128)S(1)}, f32[640,128]{1,0:T(8,128)S(1)}) custom-call(s32[1]{0:T(128)} %bitcast.32.core_ref, f32[1024,512]{1,0:T(8,128)S(1)} %get-tuple-element.42.p_ref), custom_call_target="tpu_custom_call" | custom-call | flops 300000000 | bytes 1000000 | tf_op jit(solution)/shard_map/gram/pallas_call | solution.py:207
  65.1 2.5 %collective-permute-start.17 = (f32[64,2048]{1,0:T(8,128)}, f32[64,2048]{1,0:T(8,128)}, u32[]{:S(2)}, u32[]{:S(2)}) collective-permute-start(f32[64,2048]{1,0:T(8,128)} %get-tuple-element.40), channel_id=1, source_target_pairs={{0,96},{16,112},{32,64},{48,80},{64,32},{80,48},{96,0},{112,16},{1... | collective-permute-start | bytes 1572872 | tf_op jit(solution)/shard_map/ppermute | solution.py:225
  68.4 1.8 %collective-permute-start.23 = (f32[320,128]{1,0:T(8,128)S(1)}, f32[320,128]{1,0:T(8,128)}, u32[]{:S(2)}, u32[]{:S(2)}) collective-permute-start(f32[320,128]{1,0:T(8,128)S(1)} %get-tuple-element.64), channel_id=1, source_target_pairs={{0,96},{16,112},{32,64},{48,80},{64,32},{80,48},{96,0},{112,16},{1... | collective-permute-start | bytes 491528 | tf_op jit(solution)/shard_map/ppermute | solution.py:225
  70.5 3.5 %collective-permute-done.21 = f32[320,128]{1,0:T(8,128)} collective-permute-done((f32[320,128]{1,0:T(8,128)}, f32[320,128]{1,0:T(8,128)}, u32[]{:S(2)}, u32[]{:S(2)}) %collective-permute-start.21) | collective-permute-done | bytes 163872 | tf_op jit(solution)/shard_map/ppermute | solution.py:225
  74.1 9.4 %collective-permute-done.23 = f32[320,128]{1,0:T(8,128)} collective-permute-done((f32[320,128]{1,0:T(8,128)S(1)}, f32[320,128]{1,0:T(8,128)}, u32[]{:S(2)}, u32[]{:S(2)}) %collective-permute-start.23) | collective-permute-done | bytes 163872 | tf_op jit(solution)/shard_map/ppermute | solution.py:225
  83.5 1.2 slice_add_fusion.5
  84.7 2.6 %collective-permute-start.22 = (f32[320,128]{1,0:T(8,128)S(1)}, f32[320,128]{1,0:T(8,128)S(1)}, u32[]{:S(2)}, u32[]{:S(2)}) collective-permute-start(f32[320,128]{1,0:T(8,128)S(1)} %get-tuple-element.61), channel_id=1, source_target_pairs={{0,96},{16,112},{32,64},{48,80},{64,32},{80,48},{96,0},{112,16},{1... | collective-permute-start | bytes 491528 | tf_op jit(solution)/shard_map/ppermute | solution.py:225
  87.3 1.0 slice_add_fusion
  88.2 1.5 %collective-permute-start.18 = (f32[32,2048]{1,0:T(8,128)S(1)}, f32[32,2048]{1,0:T(8,128)S(1)}, u32[]{:S(2)}, u32[]{:S(2)}) collective-permute-start(f32[32,2048]{1,0:T(8,128)S(1)} %slice_add_fusion), channel_id=1, source_target_pairs={{0,32},{16,48},{32,0},{48,16},{64,96},{80,112},{96,64},{112,80},{1... | collective-permute-start | bytes 786440 | tf_op jit(solution)/shard_map/ppermute | solution.py:225
  90.8 1.0 collective-permute-done.24
  91.8 4.0 %collective-permute-start.25 = (f32[640,128]{1,0:T(8,128)S(1)}, f32[640,128]{1,0:T(8,128)S(1)}, u32[]{:S(2)}, u32[]{:S(2)}) collective-permute-start(f32[640,128]{1,0:T(8,128)S(1)} %pad_maximum_fusion.3), channel_id=1, source_target_pairs={{0,16},{16,0},{32,48},{48,32},{64,80},{80,64},{96,112},{112,96},{1... | collective-permute-start | bytes 983048 | tf_op jit(solution)/shard_map/ppermute | solution.py:225
  95.8 1.6 %collective-permute-done.18 = f32[32,2048]{1,0:T(8,128)S(1)} collective-permute-done((f32[32,2048]{1,0:T(8,128)S(1)}, f32[32,2048]{1,0:T(8,128)S(1)}, u32[]{:S(2)}, u32[]{:S(2)}) %collective-permute-start.18) | collective-permute-done | bytes 262176 | tf_op jit(solution)/shard_map/ppermute | solution.py:225
  97.3 1.0 fusion
  99.8 3.6 %factor.4.refs_0_.w0 = f32[128,640]{1,0:T(8,128)S(1)} custom-call(f32[1280,128]{1,0:T(8,128)S(1)} %pad_maximum_fusion.refs_0_.refs_1_.refs_2_.refs_3_), custom_call_target="tpu_custom_call" | custom-call | flops 300000000 | bytes 1000000 | tf_op jit(solution)/shard_map/factor/pallas_call | solution.py:127
  103.4 4.0 %factor.5.refs_1_.w1 = f32[128,640]{1,0:T(8,128)S(1)} custom-call(f32[128,640]{1,0:T(8,128)S(1)} %factor.4.refs_0_.w0, f32[1280,128]{1,0:T(8,128)S(1)} %pad_maximum_fusion.refs_0_.refs_1_.refs_2_.refs_3_), custom_call_target="tpu_custom_call" | custom-call | flops 300000000 | bytes 1000000 | tf_op jit(solution)/shard_map/factor/pallas_call | solution.py:127
  108.3 2.0 %collective-permute-start.27 = (f32[64,2048]{1,0:T(8,128)S(1)}, f32[64,2048]{1,0:T(8,128)S(1)}, u32[]{:S(2)}, u32[]{:S(2)}) collective-permute-start(f32[64,2048]{1,0:T(8,128)S(1)} %pad_maximum_fusion.2.refs_2_), channel_id=1, source_target_pairs={{0,96},{16,112},{32,64},{48,80},{64,32},{80,48},{96,0},{112,16},{1... | collective-permute-start | bytes 1572872 | tf_op jit(solution)/shard_map/ppermute | solution.py:225
  110.3 3.3 %collective-permute-start.28 = (f32[64,2048]{1,0:T(8,128)S(1)}, f32[64,2048]{1,0:T(8,128)S(1)}, u32[]{:S(2)}, u32[]{:S(2)}) collective-permute-start(f32[64,2048]{1,0:T(8,128)S(1)} %pad_maximum_fusion.1.refs_0_), channel_id=1, source_target_pairs={{0,16},{16,0},{32,48},{48,32},{64,80},{80,64},{96,112},{112,96},{1... | collective-permute-start | bytes 1572872 | tf_op jit(solution)/shard_map/ppermute | solution.py:225
  113.6 4.1 %factor.6.refs_2_.w2 = f32[128,640]{1,0:T(8,128)S(1)} custom-call(f32[128,640]{1,0:T(8,128)S(1)} %factor.4.refs_0_.w0, f32[128,640]{1,0:T(8,128)S(1)} %factor.5.refs_1_.w1, f32[1280,128]{1,0:T(8,128)S(1)} %pad_maximum_fusion.refs_0_.refs_1_.refs_2_.refs_3_), custom_call_target="tpu_custom_call" | custom-call | flops 300000000 | bytes 1000000 | tf_op jit(solution)/shard_map/factor/pallas_call | solution.py:127
  117.7 4.2 %factor.7.w3 = f32[128,640]{1,0:T(8,128)S(1)} custom-call(f32[128,640]{1,0:T(8,128)S(1)} %factor.4.refs_0_.w0, f32[128,640]{1,0:T(8,128)S(1)} %factor.5.refs_1_.w1, f32[128,640]{1,0:T(8,128)S(1)} %factor.6.refs_2_.w2, f32[1280,128]{1,0:T(8,128)S(1)} %pad_maximum_fusion.refs_0_.refs_1_.refs_2_.refs_3_), custom_call_target="tpu_custom_call" | custom-call | flops 300000000 | bytes 1000000 | tf_op jit(solution)/shard_map/factor/pallas_call | solution.py:127
  121.9 3.0 %prepare.1 = (f32[512,512]{1,0:T(8,128)}, bf16[512,512]{1,0:T(8,128)(2,1)S(1)}, bf16[512,512]{1,0:T(8,128)(2,1)S(1)}, bf16[1024,512]{1,0:T(8,128)(2,1)S(1)}, bf16[1024,512]{1,0:T(8,128)(2,1)S(1)}) custom-call(f32[128,640]{1,0:T(8,128)S(1)} %factor.4.refs_0_.w0, f32[128,640]{1,0:T(8,128)S(1)} %factor.5.refs_1_.w1, f32[128,640]{1,0:T(8,128)S(1)} %factor.6.refs_2_.w2, ...), custom_call_target="tpu_custom_call" | custom-call | flops 300000000 | bytes 1000000 | tf_op jit(solution)/shard_map/prepare/pallas_call | solution.py:298
  124.9 1.0 copy-done.1
  125.9 1.0 copy-done.2
  127.5 1.4 collective-permute-done.29.refs_5_
  129.7 22.0 %finish.1 = (f32[512,2048]{1,0:T(8,128)}, f32[1024,2048]{1,0:T(8,128)}) custom-call(s32[16]{0:T(128)S(1)} %stack.134.table_ref, f32[64,2048]{1,0:T(8,128)S(1)} %pad_maximum_fusion.1.refs_0_, f32[64,2048]{1,0:T(8,128)S(1)} %collective-permute-done.26.refs_1_, f32[64,2048]{1,0:T(8,128)S(1)} %pad_maximum_fusion.2.refs_2_, ...), custom_call_target="tpu_custom_call" | custom-call | tf_op jit(solution)/shard_map/finish/pallas_call | solution.py:327
  (68 shorter events, 12.1 us)
Async XLA Ops:
  1.5 6.2 %collective-permute-start.2 = (f32[64,256]{1,0:T(8,128)S(1)}, f32[64,256]{1,0:T(8,128)S(1)}, u32[]{:S(2)}, u32[]{:S(2)}) collective-permute-start(f32[64,256]{1,0:T(8,128)S(1)} %get-tuple-element.66), channel_id=1, source_target_pairs={{0,2},{1,3},{2,0},{3,1},{4,6},{5,7},{6,4},{7,5},{8,10},{9,11},{10,... | collective-permute-start | bytes 196616 | tf_op jit(solution)/shard_map/ppermute | solution.py:161
  6.0 3.5 %collective-permute-start.1 = (f32[64,256]{1,0:T(8,128)S(1)}, f32[64,256]{1,0:T(8,128)S(1)}, u32[]{:S(2)}, u32[]{:S(2)}) collective-permute-start(f32[64,256]{1,0:T(8,128)S(1)} %get-tuple-element.66), channel_id=1, source_target_pairs={{0,3},{1,0},{2,1},{3,2},{4,7},{5,4},{6,5},{7,6},{8,11},{9,8},{10,9... | collective-permute-start | bytes 196616 | tf_op jit(solution)/shard_map/ppermute | solution.py:161
  6.5 4.3 %collective-permute-start = (f32[64,256]{1,0:T(8,128)S(1)}, f32[64,256]{1,0:T(8,128)S(1)}, u32[]{:S(2)}, u32[]{:S(2)}) collective-permute-start(f32[64,256]{1,0:T(8,128)S(1)} %get-tuple-element.66), channel_id=1, source_target_pairs={{0,1},{1,2},{2,3},{3,0},{4,5},{5,6},{6,7},{7,4},{8,9},{9,10},{10,1... | collective-permute-start | bytes 196616 | tf_op jit(solution)/shard_map/ppermute | solution.py:161
  10.8 15.0 %collective-permute-start.5 = (f32[256,256]{1,0:T(8,128)S(1)}, f32[256,256]{1,0:T(8,128)S(1)}, u32[]{:S(2)}, u32[]{:S(2)}) collective-permute-start(f32[256,256]{1,0:T(8,128)S(1)} %pad_maximum_fusion.4.refs_0_), channel_id=1, source_target_pairs={{0,8},{1,9},{2,10},{3,11},{4,12},{5,13},{6,14},{7,15},{8,0},{9,1},... | collective-permute-start | bytes 786440 | tf_op jit(solution)/shard_map/ppermute | solution.py:161
  13.8 5.6 %collective-permute-start.8 = (f32[64,256]{1,0:T(8,128)S(1)}, f32[64,256]{1,0:T(8,128)S(1)}, u32[]{:S(2)}, u32[]{:S(2)}) collective-permute-start(f32[64,256]{1,0:T(8,128)S(1)} %get-tuple-element.65), channel_id=1, source_target_pairs={{0,8},{1,9},{2,10},{3,11},{4,12},{5,13},{6,14},{7,15},{8,0},{9,1},... | collective-permute-start | bytes 196616 | tf_op jit(solution)/shard_map/ppermute | solution.py:161
  13.9 7.1 %collective-permute-start.7 = (f32[64,256]{1,0:T(8,128)S(1)}, f32[64,256]{1,0:T(8,128)S(1)}, u32[]{:S(2)}, u32[]{:S(2)}) collective-permute-start(f32[64,256]{1,0:T(8,128)S(1)} %get-tuple-element.65), channel_id=1, source_target_pairs={{0,12},{1,13},{2,14},{3,15},{4,0},{5,1},{6,2},{7,3},{8,4},{9,5},{1... | collective-permute-start | bytes 196616 | tf_op jit(solution)/shard_map/ppermute | solution.py:161
  16.6 6.5 %collective-permute-start.6 = (f32[64,256]{1,0:T(8,128)S(1)}, f32[64,256]{1,0:T(8,128)S(1)}, u32[]{:S(2)}, u32[]{:S(2)}) collective-permute-start(f32[64,256]{1,0:T(8,128)S(1)} %get-tuple-element.65), channel_id=1, source_target_pairs={{0,4},{1,5},{2,6},{3,7},{4,8},{5,9},{6,10},{7,11},{8,12},{9,13},{1... | collective-permute-start | bytes 196616 | tf_op jit(solution)/shard_map/ppermute | solution.py:161
  16.6 10.6 %collective-permute-start.4 = (f32[256,256]{1,0:T(8,128)S(1)}, f32[256,256]{1,0:T(8,128)S(1)}, u32[]{:S(2)}, u32[]{:S(2)}) collective-permute-start(f32[256,256]{1,0:T(8,128)S(1)} %pad_maximum_fusion.4.refs_0_), channel_id=1, source_target_pairs={{0,12},{1,13},{2,14},{3,15},{4,0},{5,1},{6,2},{7,3},{8,4},{9,5},{1... | collective-permute-start | bytes 786440 | tf_op jit(solution)/shard_map/ppermute | solution.py:161
  19.4 7.8 %collective-permute-start.3 = (f32[256,256]{1,0:T(8,128)S(1)}, f32[256,256]{1,0:T(8,128)S(1)}, u32[]{:S(2)}, u32[]{:S(2)}) collective-permute-start(f32[256,256]{1,0:T(8,128)S(1)} %pad_maximum_fusion.4.refs_0_), channel_id=1, source_target_pairs={{0,4},{1,5},{2,6},{3,7},{4,8},{5,9},{6,10},{7,11},{8,12},{9,13},{1... | collective-permute-start | bytes 786440 | tf_op jit(solution)/shard_map/ppermute | solution.py:161
  23.1 6.8 %collective-permute-start.11 = (f32[256,256]{1,0:T(8,128)S(1)}, f32[256,256]{1,0:T(8,128)S(1)}, u32[]{:S(2)}, u32[]{:S(2)}) collective-permute-start(f32[256,256]{1,0:T(8,128)S(1)} %pad_maximum_fusion.5.refs_4_), channel_id=1, source_target_pairs={{0,2},{1,3},{2,0},{3,1},{4,6},{5,7},{6,4},{7,5},{8,10},{9,11},{10,... | collective-permute-start | bytes 786440 | tf_op jit(solution)/shard_map/ppermute | solution.py:161
  24.6 9.5 %collective-permute-start.10 = (f32[256,256]{1,0:T(8,128)S(1)}, f32[256,256]{1,0:T(8,128)S(1)}, u32[]{:S(2)}, u32[]{:S(2)}) collective-permute-start(f32[256,256]{1,0:T(8,128)S(1)} %pad_maximum_fusion.5.refs_4_), channel_id=1, source_target_pairs={{0,3},{1,0},{2,1},{3,2},{4,7},{5,4},{6,5},{7,6},{8,11},{9,8},{10,9... | collective-permute-start | bytes 786440 | tf_op jit(solution)/shard_map/ppermute | solution.py:161
  25.8 9.0 %collective-permute-start.9 = (f32[256,256]{1,0:T(8,128)S(1)}, f32[256,256]{1,0:T(8,128)S(1)}, u32[]{:S(2)}, u32[]{:S(2)}) collective-permute-start(f32[256,256]{1,0:T(8,128)S(1)} %pad_maximum_fusion.5.refs_4_), channel_id=1, source_target_pairs={{0,1},{1,2},{2,3},{3,0},{4,5},{5,6},{6,7},{7,4},{8,9},{9,10},{10,1... | collective-permute-start | bytes 786440 | tf_op jit(solution)/shard_map/ppermute | solution.py:161
  29.9 0.7 copy-start.3
  34.1 0.7 copy-start.5
  34.8 0.7 copy-start.7
  35.5 0.9 copy-start.4
  36.5 0.9 copy-start.6
  37.4 0.9 copy-start.8
  39.9 3.4 %copy-start = (f32[1024,2048]{1,0:T(8,128)S(1)}, f32[1024,2048]{1,0:T(8,128)}, u32[]{:S(2)}) copy-start(f32[1024,2048]{1,0:T(8,128)} %refs_12_.1) | copy-start | bytes 25165828
  52.5 6.5 %collective-permute-start.12 = (f32[256,1024]{1,0:T(8,128)S(1)}, f32[256,1024]{1,0:T(8,128)S(1)}, u32[]{:S(2)}, u32[]{:S(2)}) collective-permute-start(f32[256,1024]{1,0:T(8,128)S(1)} %get-tuple-element.35), channel_id=1, source_target_pairs={{0,16},{16,0},{32,48},{48,32},{64,80},{80,64},{96,112},{112,96},{1... | collective-permute-start | bytes 3145736 | tf_op jit(solution)/shard_map/ppermute | solution.py:225
  56.8 3.8 %collective-permute-start.13 = (f32[256,1024]{1,0:T(8,128)S(1)}, f32[256,1024]{1,0:T(8,128)S(1)}, u32[]{:S(2)}, u32[]{:S(2)}) collective-permute-start(f32[256,1024]{1,0:T(8,128)S(1)} %get-tuple-element.36), channel_id=1, source_target_pairs={{0,16},{16,0},{32,48},{48,32},{64,80},{80,64},{96,112},{112,96},{1... | collective-permute-start | bytes 3145736 | tf_op jit(solution)/shard_map/ppermute | solution.py:225
  61.6 6.0 %copy-start.9 = (f32[64,2048]{1,0:T(8,128)}, f32[64,2048]{1,0:T(8,128)S(1)}, u32[]{:S(2)}) copy-start(f32[64,2048]{1,0:T(8,128)S(1)} %get-tuple-element.38) | copy-start | bytes 1572868
  64.6 2.9 %collective-permute-start.20 = (f32[640,128]{1,0:T(8,128)S(1)}, f32[640,128]{1,0:T(8,128)S(1)}, u32[]{:S(2)}, u32[]{:S(2)}) collective-permute-start(f32[640,128]{1,0:T(8,128)S(1)} %get-tuple-element.44), channel_id=1, source_target_pairs={{0,16},{16,0},{32,48},{48,32},{64,80},{80,64},{96,112},{112,96},{1... | collective-permute-start | bytes 983048 | tf_op jit(solution)/shard_map/ppermute | solution.py:225
  65.1 22.2 %collective-permute-start.17 = (f32[64,2048]{1,0:T(8,128)}, f32[64,2048]{1,0:T(8,128)}, u32[]{:S(2)}, u32[]{:S(2)}) collective-permute-start(f32[64,2048]{1,0:T(8,128)} %get-tuple-element.40), channel_id=1, source_target_pairs={{0,96},{16,112},{32,64},{48,80},{64,32},{80,48},{96,0},{112,16},{1... | collective-permute-start | bytes 1572872 | tf_op jit(solution)/shard_map/ppermute | solution.py:225
  67.6 0.8 copy-start.10
  68.4 5.7 %collective-permute-start.21 = (f32[320,128]{1,0:T(8,128)}, f32[320,128]{1,0:T(8,128)}, u32[]{:S(2)}, u32[]{:S(2)}) collective-permute-start(f32[320,128]{1,0:T(8,128)} %get-tuple-element.63), channel_id=1, source_target_pairs={{0,32},{16,48},{32,0},{48,16},{64,96},{80,112},{96,64},{112,80},{1... | collective-permute-start | bytes 491528 | tf_op jit(solution)/shard_map/ppermute | solution.py:225
  68.4 15.1 %collective-permute-start.23 = (f32[320,128]{1,0:T(8,128)S(1)}, f32[320,128]{1,0:T(8,128)}, u32[]{:S(2)}, u32[]{:S(2)}) collective-permute-start(f32[320,128]{1,0:T(8,128)S(1)} %get-tuple-element.64), channel_id=1, source_target_pairs={{0,96},{16,112},{32,64},{48,80},{64,32},{80,48},{96,0},{112,16},{1... | collective-permute-start | bytes 491528 | tf_op jit(solution)/shard_map/ppermute | solution.py:225
  70.2 19.6 %collective-permute-start.14 = (f32[64,2048]{1,0:T(8,128)}, f32[64,2048]{1,0:T(8,128)S(1)}, u32[]{:S(2)}, u32[]{:S(2)}) collective-permute-start(f32[64,2048]{1,0:T(8,128)} %copy-done.9), channel_id=1, source_target_pairs={{0,32},{16,48},{32,0},{48,16},{64,96},{80,112},{96,64},{112,80},{1... | collective-permute-start | bytes 1572872 | tf_op jit(solution)/shard_map/ppermute | solution.py:225
  84.7 6.0 %collective-permute-start.22 = (f32[320,128]{1,0:T(8,128)S(1)}, f32[320,128]{1,0:T(8,128)S(1)}, u32[]{:S(2)}, u32[]{:S(2)}) collective-permute-start(f32[320,128]{1,0:T(8,128)S(1)} %get-tuple-element.61), channel_id=1, source_target_pairs={{0,96},{16,112},{32,64},{48,80},{64,32},{80,48},{96,0},{112,16},{1... | collective-permute-start | bytes 491528 | tf_op jit(solution)/shard_map/ppermute | solution.py:225
  87.2 4.5 %collective-permute-start.24 = (f32[320,128]{1,0:T(8,128)S(1)}, f32[320,128]{1,0:T(8,128)S(1)}, u32[]{:S(2)}, u32[]{:S(2)}) collective-permute-start(f32[320,128]{1,0:T(8,128)S(1)} %get-tuple-element.62), channel_id=1, source_target_pairs={{0,32},{16,48},{32,0},{48,16},{64,96},{80,112},{96,64},{112,80},{1... | collective-permute-start | bytes 491528 | tf_op jit(solution)/shard_map/ppermute | solution.py:225
  88.2 9.1 %collective-permute-start.18 = (f32[32,2048]{1,0:T(8,128)S(1)}, f32[32,2048]{1,0:T(8,128)S(1)}, u32[]{:S(2)}, u32[]{:S(2)}) collective-permute-start(f32[32,2048]{1,0:T(8,128)S(1)} %slice_add_fusion), channel_id=1, source_target_pairs={{0,32},{16,48},{32,0},{48,16},{64,96},{80,112},{96,64},{112,80},{1... | collective-permute-start | bytes 786440 | tf_op jit(solution)/shard_map/ppermute | solution.py:225
  89.8 9.3 %collective-permute-start.15 = (f32[32,2048]{1,0:T(8,128)S(1)}, f32[32,2048]{1,0:T(8,128)S(1)}, u32[]{:S(2)}, u32[]{:S(2)}) collective-permute-start(f32[32,2048]{1,0:T(8,128)S(1)} %slice_add_fusion.2), channel_id=1, source_target_pairs={{0,96},{16,112},{32,64},{48,80},{64,32},{80,48},{96,0},{112,16},{1... | collective-permute-start | bytes 786440 | tf_op jit(solution)/shard_map/ppermute | solution.py:225
  91.8 7.9 %collective-permute-start.25 = (f32[640,128]{1,0:T(8,128)S(1)}, f32[640,128]{1,0:T(8,128)S(1)}, u32[]{:S(2)}, u32[]{:S(2)}) collective-permute-start(f32[640,128]{1,0:T(8,128)S(1)} %pad_maximum_fusion.3), channel_id=1, source_target_pairs={{0,16},{16,0},{32,48},{48,32},{64,80},{80,64},{96,112},{112,96},{1... | collective-permute-start | bytes 983048 | tf_op jit(solution)/shard_map/ppermute | solution.py:225
  98.3 9.1 %collective-permute-start.19 = (f32[32,2048]{1,0:T(8,128)S(1)}, f32[32,2048]{1,0:T(8,128)S(1)}, u32[]{:S(2)}, u32[]{:S(2)}) collective-permute-start(f32[32,2048]{1,0:T(8,128)S(1)} %fusion), channel_id=1, source_target_pairs={{0,32},{16,48},{32,0},{48,16},{64,96},{80,112},{96,64},{112,80},{1... | collective-permute-start | bytes 786440 | tf_op jit(solution)/shard_map/ppermute | solution.py:225
  99.2 8.4 %collective-permute-start.16 = (f32[32,2048]{1,0:T(8,128)S(1)}, f32[32,2048]{1,0:T(8,128)S(1)}, u32[]{:S(2)}, u32[]{:S(2)}) collective-permute-start(f32[32,2048]{1,0:T(8,128)S(1)} %fusion.1), channel_id=1, source_target_pairs={{0,96},{16,112},{32,64},{48,80},{64,32},{80,48},{96,0},{112,16},{1... | collective-permute-start | bytes 786440 | tf_op jit(solution)/shard_map/ppermute | solution.py:225
  107.6 19.3 %collective-permute-start.26 = (f32[64,2048]{1,0:T(8,128)S(1)}, f32[64,2048]{1,0:T(8,128)S(1)}, u32[]{:S(2)}, u32[]{:S(2)}) collective-permute-start(f32[64,2048]{1,0:T(8,128)S(1)} %pad_maximum_fusion.1.refs_0_), channel_id=1, source_target_pairs={{0,32},{16,48},{32,0},{48,16},{64,96},{80,112},{96,64},{112,80},{1... | collective-permute-start | bytes 1572872 | tf_op jit(solution)/shard_map/ppermute | solution.py:225
  108.3 18.7 %collective-permute-start.27 = (f32[64,2048]{1,0:T(8,128)S(1)}, f32[64,2048]{1,0:T(8,128)S(1)}, u32[]{:S(2)}, u32[]{:S(2)}) collective-permute-start(f32[64,2048]{1,0:T(8,128)S(1)} %pad_maximum_fusion.2.refs_2_), channel_id=1, source_target_pairs={{0,96},{16,112},{32,64},{48,80},{64,32},{80,48},{96,0},{112,16},{1... | collective-permute-start | bytes 1572872 | tf_op jit(solution)/shard_map/ppermute | solution.py:225
  110.3 17.2 %collective-permute-start.28 = (f32[64,2048]{1,0:T(8,128)S(1)}, f32[64,2048]{1,0:T(8,128)S(1)}, u32[]{:S(2)}, u32[]{:S(2)}) collective-permute-start(f32[64,2048]{1,0:T(8,128)S(1)} %pad_maximum_fusion.1.refs_0_), channel_id=1, source_target_pairs={{0,16},{16,0},{32,48},{48,32},{64,80},{80,64},{96,112},{112,96},{1... | collective-permute-start | bytes 1572872 | tf_op jit(solution)/shard_map/ppermute | solution.py:225
  113.6 13.9 %collective-permute-start.30 = (f32[64,2048]{1,0:T(8,128)S(1)}, f32[64,2048]{1,0:T(8,128)S(1)}, u32[]{:S(2)}, u32[]{:S(2)}) collective-permute-start(f32[64,2048]{1,0:T(8,128)S(1)} %pad_maximum_fusion.2.refs_2_), channel_id=1, source_target_pairs={{0,16},{16,0},{32,48},{48,32},{64,80},{80,64},{96,112},{112,96},{1... | collective-permute-start | bytes 1572872 | tf_op jit(solution)/shard_map/ppermute | solution.py:225
  124.9 1.0 copy-start.1
  125.9 1.0 copy-start.2
  126.9 2.0 %collective-permute-start.29 = (f32[64,2048]{1,0:T(8,128)S(1)}, f32[64,2048]{1,0:T(8,128)S(1)}, u32[]{:S(2)}, u32[]{:S(2)}) collective-permute-start(f32[64,2048]{1,0:T(8,128)S(1)} %collective-permute-done.26.refs_1_), channel_id=1, source_target_pairs={{0,16},{16,0},{32,48},{48,32},{64,80},{80,64},{96,112},{112,96},{1... | collective-permute-start | bytes 1572872 | tf_op jit(solution)/shard_map/ppermute | solution.py:225
  127.4 2.3 %collective-permute-start.31 = (f32[64,2048]{1,0:T(8,128)S(1)}, f32[64,2048]{1,0:T(8,128)S(1)}, u32[]{:S(2)}, u32[]{:S(2)}) collective-permute-start(f32[64,2048]{1,0:T(8,128)S(1)} %collective-permute-done.27.refs_3_), channel_id=1, source_target_pairs={{0,16},{16,0},{32,48},{48,32},{64,80},{80,64},{96,112},{112,96},{1... | collective-permute-start | bytes 1572872 | tf_op jit(solution)/shard_map/ppermute | solution.py:225

commit v2 on v1

--- a/solution.py
+++ b/solution.py
@@ -12,7 +12,6 @@
 F32 = jnp.float32
 GROUP = 32
 TILE = 512
-NARROW = 256
 
 
 def near(i):
@@ -23,8 +22,9 @@
     return 3 - i
 
 
+PAIR = (near, far)
 CORE = [(r, r ^ 1) for r in range(8)]
-XPAIR = [[(x * 2 + c, pair(x) * 2 + c) for x in range(4) for c in range(2)] for pair in (near, far)]
+ROW = [[(x * 2 + c, PAIR[c ^ step](x) * 2 + c) for x in range(4) for c in (0, 1)] for step in (0, 1)]
 
 
 def ring_bits(i):
@@ -71,7 +71,7 @@
     )
 
 
-def params(mib=40):
+def params(mib):
     return pltpu.CompilerParams(vmem_limit_bytes=mib << 20)
 
 
@@ -130,61 +130,61 @@
         in_specs=whole(k + 1),
         out_specs=whole()[0],
         scratch_shapes=[pltpu.VMEM((128, window), F32)],
-        compiler_params=params(16),
+        compiler_params=params(8),
         cost_estimate=cheap(),
         name="factor",
     )(*earlier, packed)
 
 
-def shifts(axis):
+def gather_pairs(q, step):
     out = []
-    for by in (1, 3, 2):
-        if axis == "y":
-            out.append((by, [(y * 4 + z, (y + by) % 4 * 4 + z) for y in range(4) for z in range(4)]))
-        else:
-            out.append((by, [(y * 4 + z, y * 4 + (z + by) % 4) for y in range(4) for z in range(4)]))
+    for x in range(4):
+        for c in (0, 1):
+            for y in range(4):
+                for z in range(4):
+                    flip = PAIR[(step % 2) ^ q]
+                    to = (y, flip(z)) if (step // 2) ^ c == 0 else (flip(y), z)
+                    out.append(((x * 2 + c) * 16 + y * 4 + z, (x * 2 + c) * 16 + to[0] * 4 + to[1]))
     return out
 
 
-def gather_panel(panel):
+def gather_panel(panel, core):
     col = lax.axis_index("col")
     n = panel.shape[1] // 2
-    held = [panel[:, :n], panel[:, n:]]
+    pieces = [[panel[:, :n]], [panel[:, n:]]]
     place = [[(col // 4, col % 4)], [(col // 4, col % 4)]]
-    pieces = [None, None]
-    for step in (0, 1):
+    for step in range(4):
+        held = [p[0] if len(p) == 1 else jnp.concatenate(p, axis=0) for p in pieces]
         for q in (0, 1):
-            axis = "zy"[step ^ q]
-            pieces[q] = [held[q]]
-            known = list(place[q])
-            for by, pairs in shifts(axis):
-                pieces[q].append(lax.ppermute(held[q], "col", pairs))
-                place[q] += [((y - by) % 4, z) if axis == "y" else (y, (z - by) % 4) for y, z in known]
-        if step == 0:
-            held = [jnp.concatenate(p, axis=0) for p in pieces]
+            pieces[q] = [held[q], lax.ppermute(held[q], ("row", "col"), gather_pairs(q, step))]
+            flip = PAIR[(step % 2) ^ q]
+            along_z = core == step // 2
+            place[q] = place[q] + [
+                (jnp.where(along_z, y, flip(y)), jnp.where(along_z, flip(z), z)) for y, z in place[q]
+            ]
     return pieces[0] + pieces[1], [y * 4 + z for q in (0, 1) for y, z in place[q]]
 
 
 def turn_kernel(order_ref, *refs):
-    pieces, (o_ref, hi_ref, lo_ref) = refs[:8], refs[8:]
+    pieces, (o_ref, hi_ref, lo_ref) = refs[:4], refs[4:]
     for i, ref in enumerate(pieces):
-        q, four = divmod(i, 4)
-        for p in range(4):
-            at = pl.multiple_of(order_ref[i * 4 + p] * 64, 64)
+        q = i // 2
+        for p in range(8):
+            at = pl.multiple_of(order_ref[i * 8 + p] * 64, 64)
             o_ref[pl.ds(at, 64), q * 256:q * 256 + 256] = ref[p * 64:p * 64 + 64, :]
     for j in range(0, 1024, 128):
         hi_ref[:, j:j + 128], lo_ref[:, j:j + 128] = split(jnp.transpose(o_ref[j:j + 128, :]))
 
 
 def turn(pieces, order):
-    depth, b = pieces[0].shape[0] * 4, pieces[0].shape[1] * 2
+    depth, b = pieces[0].shape[0] * 2, pieces[0].shape[1] * 2
     out = jax.ShapeDtypeStruct((b, depth), BF16)
     return pl.pallas_call(
         turn_kernel,
         out_shape=(jax.ShapeDtypeStruct((depth, b), F32), out, out),
-        in_specs=[SCALARS] + whole(8),
+        in_specs=[SCALARS] + whole(4),
         out_specs=whole(3),
-        compiler_params=params(),
+        compiler_params=params(12),
         cost_estimate=cheap(),
         name="turn",
     )(jnp.stack(order).astype(jnp.int32), *pieces)
@@ -210,7 +210,7 @@
         in_specs=[SCALARS] + whole(),
         out_specs=whole(2),
         scratch_shapes=[pltpu.VMEM((1280, 128), F32)],
-        compiler_params=params(),
+        compiler_params=params(12),
         cost_estimate=cheap(),
         name="gram",
     )(core.reshape(1).astype(jnp.int32), rows)
@@ -227,9 +227,9 @@
 
 def share_kernel(table_ref, hi_ref, lo_ref, t_ref, keep_ref, give_ref, total):
     got = dot3((hi_ref[...], lo_ref[...]), split(t_ref[...]))
-    for p in range(16):
-        at = pl.multiple_of(table_ref[p] * 32, 32)
-        total[pl.ds(at, 32), :] = got[p * 32:p * 32 + 32, :]
+    for p in range(8):
+        at = pl.multiple_of(table_ref[p] * 64, 64)
+        total[pl.ds(at, 64), :] = got[p * 64:p * 64 + 64, :]
     keep_ref[...] = total[:256, :]
     give_ref[...] = total[256:, :]
 
@@ -245,27 +245,27 @@
         in_specs=[SCALARS] + whole(2) + [pl.BlockSpec((depth, TILE), lambda i: (0, i + first // TILE))],
         out_specs=(out, out),
         scratch_shapes=[pltpu.VMEM((512, TILE), F32)],
-        compiler_params=params(),
+        compiler_params=params(58),
         cost_estimate=cheap(),
         name="share",
     )(table, hi, lo, trailing)
 
 
-def fold_kernel(k0, k1, g0, g1, a_give, b_give, a_keep, b_keep):
+def fold_kernel(k0, k1, g0, g1, keep_ref, give_ref):
     n = k0.shape[1]
     for cols, k, g in ((slice(0, n), k0, g0), (slice(n, 2 * n), k1, g1)):
-        for at, ref in ((64, a_give), (192, b_give), (0, a_keep), (128, b_keep)):
-            ref[:, cols] = k[at:at + 64, :] + g[at:at + 64, :]
+        give_ref[:, cols] = k[128:, :] + g[128:, :]
+        keep_ref[:, cols] = k[:128, :] + g[:128, :]
 
 
 def fold(keeps, gots):
-    out = jax.ShapeDtypeStruct((64, 2 * keeps[0].shape[1]), F32)
+    out = jax.ShapeDtypeStruct((128, 2 * keeps[0].shape[1]), F32)
     return pl.pallas_call(
         fold_kernel,
-        out_shape=(out,) * 4,
+        out_shape=(out, out),
         in_specs=whole(4),
-        out_specs=whole(4),
-        compiler_params=params(),
+        out_specs=whole(2),
+        compiler_params=params(12),
         cost_estimate=cheap(),
         name="fold",
     )(*keeps, *gots)
@@ -301,18 +301,17 @@
         in_specs=whole(5),
         out_specs=whole(5),
         scratch_shapes=[pltpu.VMEM(square, F32)],
-        compiler_params=params(),
+        compiler_params=params(16),
         cost_estimate=cheap(),
         name="prepare",
     )(*factors, rows)
 
 
 def finish_kernel(table_ref, *refs):
-    pieces, (ihi, ilo, bhi, blo, t_ref, c_ref, o_ref, total) = refs[:8], refs[8:]
+    pieces, (ihi, ilo, bhi, blo, t_ref, c_ref, o_ref, total) = refs[:4], refs[4:]
     for p in range(8):
-        for half in (0, 1):
-            at = pl.multiple_of(table_ref[2 * p + half] * 32, 32)
-            total[pl.ds(at, 32), :] = pieces[p][half * 32:half * 32 + 32, :]
+        at = pl.multiple_of(table_ref[p] * 64, 64)
+        total[pl.ds(at, 64), :] = pieces[p // 2][p % 2 * 64:p % 2 * 64 + 64, :]
     coupling = dot3((ihi[...], ilo[...]), split(total[...]))
     c_ref[...] = coupling
     c = split(coupling)
@@ -327,14 +326,14 @@
     return pl.pallas_call(
         finish_kernel,
         out_shape=(jax.ShapeDtypeStruct((b, width), F32), jax.ShapeDtypeStruct((depth, width), F32)),
-        grid=(width // NARROW,),
+        grid=(width // TILE,),
         in_specs=[SCALARS]
-        + [pl.BlockSpec((64, NARROW), lambda i: (0, i))] * 8
+        + [pl.BlockSpec((128, TILE), lambda i: (0, i))] * 4
         + whole(4)
-        + [pl.BlockSpec((depth, NARROW), lambda i: (0, i))],
-        out_specs=(pl.BlockSpec((b, NARROW), lambda i: (0, i)), pl.BlockSpec((depth, NARROW), lambda i: (0, i))),
-        scratch_shapes=[pltpu.VMEM((b, NARROW), F32)],
-        compiler_params=params(48),
+        + [pl.BlockSpec((depth, TILE), lambda i: (0, i))],
+        out_specs=(pl.BlockSpec((b, TILE), lambda i: (0, i)), pl.BlockSpec((depth, TILE), lambda i: (0, i))),
+        scratch_shapes=[pltpu.VMEM((b, TILE), F32)],
+        compiler_params=params(58),
         name="finish",
     )(table, *pieces, ihi, ilo, bhi, blo, trailing)
 
@@ -347,45 +346,39 @@
     row = lax.axis_index("row")
     core = row % 2
     bits = ring_bits(row // 2)
-    pieces, order = gather_panel(panel)
+    pieces, order = gather_panel(panel, core)
     rows, hi, lo = turn(pieces, order)
 
-    def held(half, part, i, j):
-        s, t = (bits[0], bits[1]) if part == 0 else (bits[1], bits[0])
-        return (half ^ core) * 8 + part * 4 + (i ^ s) * 2 + (j ^ t)
-
-    spots = [held(half, part, i, j) for half in (0, 1) for part in (0, 1) for i in (0, 1) for j in (0, 1)]
-    table = jnp.stack(spots).astype(jnp.int32)
+    def held(half, i, j):
+        owner = half ^ core
+        return owner * 4 + (i ^ jnp.where(owner == 0, bits[0], bits[1])) * 2 + (j ^ jnp.where(owner == 0, bits[1], bits[0]))
+
+    table = jnp.stack([held(half, i, j) for half in (0, 1) for i in (0, 1) for j in (0, 1)]).astype(jnp.int32)
+    inverse = jnp.zeros_like(table).at[table].set(jnp.arange(8, dtype=jnp.int32))
     width = trailing.shape[1] // 2
-    keep, give = zip(*[share(table, hi, lo, trailing, at, width) for at in (0, width)])
-    got = [swap(g, CORE) for g in give]
-    a_give, b_give, a_keep, b_keep = fold(keep, got)
-
-    came = [swap(g, XPAIR[h]) for h, g in ((0, a_give), (1, b_give))]
-    gram_keep, gram_give = gram_share(after(rows, a_give), core)
+    keep, give = zip(*[share(inverse, hi, lo, trailing, at, width) for at in (0, width)])
+    keep, give = fold(keep, [swap(g, CORE) for g in give])
+
+    came = swap(give, ROW[0])
+    gram_keep, gram_give = gram_share(after(rows, give), core)
     gram = gram_keep + swap(gram_give, CORE)
-    n = gram.shape[0] // 2
-    one, two = gram[:n], gram[n:]
-    one, two = one + swap(one, XPAIR[0]), two + swap(two, XPAIR[1])
-
-    parts = [(k[:32] + c[:32], k[32:] + c[32:]) for k, c in zip((a_keep, b_keep), came)]
-    came = [swap(parts[h][1], XPAIR[1 - h]) for h in (0, 1)]
-    one, two = one + swap(one, XPAIR[1]), two + swap(two, XPAIR[0])
-    gram = jnp.concatenate([one, two], axis=0)
+    gram = gram + swap(gram, ROW[0])
+    give, keep = keep[64:] + came[64:], keep[:64] + came[:64]
+    came = swap(give, ROW[1])
+    gram = gram + swap(gram, ROW[1])
     packed = join(gram, swap(gram, CORE), core)
-
-    own = [parts[h][0] + came[h] for h in (0, 1)]
-    came = [swap(own[h], XPAIR[1 - h]) for h in (0, 1)]
+    own = keep + came
+    came = swap(own, ROW[1])
     factors = [factor_rows(0, 4, [], packed)]
     factors.append(factor_rows(1, 4, factors, packed))
-    own = [jnp.concatenate([own[h], came[h]], axis=0) for h in (0, 1)]
+    own = jnp.concatenate([own, came], axis=0)
     own, factors = lax.optimization_barrier((own, factors))
-    came = [swap(own[h], XPAIR[h]) for h in (0, 1)]
+    came = swap(own, ROW[0])
     factors.append(factor_rows(2, 4, factors, packed))
     factors.append(factor_rows(3, 4, factors, packed))
     r_factor, ihi, ilo, bhi, blo = prepare(factors, rows)
     came, ihi = lax.optimization_barrier((came, ihi))
-    mine = [own[0], came[0], own[1], came[1]]
+    mine = [own, came]
     theirs = [swap(p, CORE) for p in mine]
     coupling, out = finish(table, mine + theirs, ihi, ilo, bhi, blo, trailing)
     return (r_factor, coupling, out)

time: 152 us -> 133 us (0.88)
  starting transfers between devices: 44.4 us -> 30.6 us
  other arithmetic: 3.59 us -> 0.59 us
  local copies, waits for them, and re-layouts: 12.2 us -> 9.53 us
  waiting for transfers between devices: 34.9 us -> 37.5 us
  Pallas kernels: 55.8 us -> 53.5 us
    ppermute x20 -> x12, starting transfers between devices: 25.8 us -> 15.9 us  [swap(): return lax.ppermute(a, 'row', pairs)]
    pallas_call x1, Pallas kernels: 22 us -> 15.7 us  [finish(): pl.pallas_call(finish_kernel, out_shape=(jax.ShapeDtypeStruct((b, width),...]
    ppermute x20 -> x12, waiting for transfers between devices: 21.9 us -> 26.8 us  [swap(): return lax.ppermute(a, 'row', pairs)]
    pallas_call x2, Pallas kernels: 9.28 us -> 14 us  [share(): pl.pallas_call(share_kernel, out_shape=(half, half), grid=(width // TILE,...]
    ppermute x12 -> x8, starting transfers between devices: 18.6 us -> 14.7 us  [gather_panel(): lax.ppermute(held[q], ('row', 'col'), gather_pairs(q, step))]
    unnamed x22 -> x24, local copies, waits for them, and re-layouts: 10.3 us -> 6.76 us
    add x7 -> x4, other arithmetic: 3.31 us -> 0.26 us  [the longest x1 0.11 us: local(): own = keep + came]
    ppermute x12 -> x8, waiting for transfers between devices: 13.1 us -> 10.7 us  [gather_panel(): lax.ppermute(held[q], ('row', 'col'), gather_pairs(q, step))]
  transfers between devices with their start and end apart: 32 -> 20, of which waited for: 18 -> 13; matrix products, arithmetic and copies ran while one was open for 3% -> 2% of each run, Pallas kernels for 13% -> 17%
where the time goes in v2:
time: 133 us
  Pallas kernels  53.5 us (40%)
  waiting for transfers between devices  37.5 us (28%)
  starting transfers between devices  30.6 us (23%)
  local copies, waits for them, and re-layouts  9.53 us (7%)
    ppermute x12, waiting for transfers between devices, swap(): return lax.ppermute(a, 'row', pairs)  26.8 us
    pallas_call x4, Pallas kernels, factor_rows(): pl.pallas_call(functools.partial(factor_kernel, k, nb), out_shape=jax.Sha...  16 us
    ppermute x12, starting transfers between devices, swap(): return lax.ppermute(a, 'row', pairs)  15.9 us
    pallas_call x1, Pallas kernels, finish(): pl.pallas_call(finish_kernel, out_shape=(jax.ShapeDtypeStruct((b, width),...  15.7 us
    ppermute x8, starting transfers between devices, gather_panel(): lax.ppermute(held[q], ('row', 'col'), gather_pairs(q, step))  14.7 us
    pallas_call x2, Pallas kernels, share(): pl.pallas_call(share_kernel, out_shape=(half, half), grid=(width // TILE,...  14 us
    ppermute x8, waiting for transfers between devices, gather_panel(): lax.ppermute(held[q], ('row', 'col'), gather_pairs(q, step))  10.7 us
    unnamed x24, local copies, waits for them, and re-layouts  6.76 us
  transfers between devices with their start and end apart: 20, of which 13 were waited for; matrix products, arithmetic and copies ran while one was open for 2% of the time, Pallas kernels for 17%

profile of v2, /device:TPU:1, one launch (start us, length us, event | category | flops | bytes accessed | tf_op | source)
XLA Modules:
  0.0 132.7 jit_solution(11935642786317114745)
XLA Ops:
  0.6 0.9 fusion.4
  1.5 2.2 %collective-permute-start = (f32[64,256]{1,0:T(8,128)S(1)}, f32[64,256]{1,0:T(8,128)S(1)}, u32[]{:S(2)}, u32[]{:S(2)}) collective-permute-start(f32[64,256]{1,0:T(8,128)S(1)} %get-tuple-element.54), channel_id=1, source_target_pairs={{0,1},{1,0},{2,3},{3,2},{4,5},{5,4},{6,7},{7,6},{8,9},{9,8},{10,11... | collective-permute-start | bytes 196616 | tf_op jit(solution)/shard_map/ppermute | solution.py:159
  3.7 1.9 %collective-permute-start.4 = (f32[64,256]{1,0:T(8,128)S(1)}, f32[64,256]{1,0:T(8,128)S(1)}, u32[]{:S(2)}, u32[]{:S(2)}) collective-permute-start(f32[64,256]{1,0:T(8,128)S(1)} %get-tuple-element.53), channel_id=1, source_target_pairs={{0,3},{1,2},{2,1},{3,0},{4,7},{5,6},{6,5},{7,4},{8,11},{9,10},{10,... | collective-permute-start | bytes 196616 | tf_op jit(solution)/shard_map/ppermute | solution.py:159
  5.6 2.7 %collective-permute-start.1 = (f32[128,256]{1,0:T(8,128)S(1)}, f32[128,256]{1,0:T(8,128)S(1)}, u32[]{:S(2)}, u32[]{:S(2)}) collective-permute-start(f32[128,256]{1,0:T(8,128)S(1)} %pad_maximum_fusion.6), channel_id=1, source_target_pairs={{0,3},{1,2},{2,1},{3,0},{4,7},{5,6},{6,5},{7,4},{8,11},{9,10},{10,... | collective-permute-start | bytes 393224 | tf_op jit(solution)/shard_map/ppermute | solution.py:159
  8.5 2.3 %collective-permute-done.1 = f32[128,256]{1,0:T(8,128)S(1)} collective-permute-done((f32[128,256]{1,0:T(8,128)S(1)}, f32[128,256]{1,0:T(8,128)S(1)}, u32[]{:S(2)}, u32[]{:S(2)}) %collective-permute-start.1) | collective-permute-done | bytes 131104 | tf_op jit(solution)/shard_map/ppermute | solution.py:159
  10.8 1.7 %collective-permute-start.2 = (f32[256,256]{1,0:T(8,128)S(1)}, f32[256,256]{1,0:T(8,128)S(1)}, u32[]{:S(2)}, u32[]{:S(2)}) collective-permute-start(f32[256,256]{1,0:T(8,128)S(1)} %pad_maximum_fusion.4), channel_id=1, source_target_pairs={{0,4},{1,5},{2,6},{3,7},{4,0},{5,1},{6,2},{7,3},{8,12},{9,13},{10,... | collective-permute-start | bytes 786440 | tf_op jit(solution)/shard_map/ppermute | solution.py:159
  12.5 3.9 %collective-permute-start.6 = (f32[256,256]{1,0:T(8,128)S(1)}, f32[256,256]{1,0:T(8,128)S(1)}, u32[]{:S(2)}, u32[]{:S(2)}) collective-permute-start(f32[256,256]{1,0:T(8,128)S(1)} %pad_maximum_fusion.5), channel_id=1, source_target_pairs={{0,12},{1,13},{2,14},{3,15},{4,8},{5,9},{6,10},{7,11},{8,4},{9,5},... | collective-permute-start | bytes 786440 | tf_op jit(solution)/shard_map/ppermute | solution.py:159
  16.4 1.5 %collective-permute-done.2 = f32[256,256]{1,0:T(8,128)S(1)} collective-permute-done((f32[256,256]{1,0:T(8,128)S(1)}, f32[256,256]{1,0:T(8,128)S(1)}, u32[]{:S(2)}, u32[]{:S(2)}) %collective-permute-start.2) | collective-permute-done | bytes 262176 | tf_op jit(solution)/shard_map/ppermute | solution.py:159
  18.0 2.0 %collective-permute-start.3 = (f32[512,256]{1,0:T(8,128)S(1)}, f32[512,256]{1,0:T(8,128)S(1)}, u32[]{:S(2)}, u32[]{:S(2)}) collective-permute-start(f32[512,256]{1,0:T(8,128)S(1)} %pad_maximum_fusion.2.refs_0_), channel_id=1, source_target_pairs={{0,12},{1,13},{2,14},{3,15},{4,8},{5,9},{6,10},{7,11},{8,4},{9,5},... | collective-permute-start | bytes 1572872 | tf_op jit(solution)/shard_map/ppermute | solution.py:159
  20.0 0.2 collective-permute-done.6
  20.7 1.1 scatter_custom_fusion.table_ref
  21.9 5.7 %collective-permute-done.3.refs_1_ = f32[512,256]{1,0:T(8,128)S(1)} collective-permute-done((f32[512,256]{1,0:T(8,128)S(1)}, f32[512,256]{1,0:T(8,128)S(1)}, u32[]{:S(2)}, u32[]{:S(2)}) %collective-permute-start.3) | collective-permute-done | bytes 524320 | tf_op jit(solution)/shard_map/ppermute | solution.py:159
  27.6 1.0 collective-permute-done.7.refs_3_
  28.6 1.4 %turn.1 = (f32[1024,512]{1,0:T(8,128)S(1)}, bf16[512,1024]{1,0:T(8,128)(2,1)S(1)}, bf16[512,1024]{1,0:T(8,128)(2,1)S(1)}) custom-call(s32[32]{0:T(128)S(1)} %stack.158.order_ref, f32[512,256]{1,0:T(8,128)S(1)} %pad_maximum_fusion.2.refs_0_, f32[512,256]{1,0:T(8,128)S(1)} %collective-permute-done.3.refs_1_, f32[512,256]{1,0:T(8,128)S(1)} %pad_maximum_fusion.3.refs_2_, ...), custom_call_target="tpu_custom_call" | custom-call | flops 300000000 | bytes 1000000 | tf_op jit(solution)/shard_map/turn/pallas_call | solution.py:182
  30.1 1.0 copy-done
  31.1 1.0 copy-done.1
  32.0 6.9 %share.3 = (f32[256,1024]{1,0:T(8,128)}, f32[256,1024]{1,0:T(8,128)}) custom-call(s32[8]{0:T(128)} %scatter_custom_fusion.table_ref, bf16[512,1024]{1,0:T(8,128)(2,1)} %copy-done, bf16[512,1024]{1,0:T(8,128)(2,1)} %copy-done.1, f32[1024,2048]{1,0:T(8,128)} %refs_8_.1), custom_call_target="tpu_custom_call" | custom-call | flops 300000000 | bytes 1000000 | tf_op jit(solution)/shard_map/share/pallas_call | solution.py:241
  39.0 7.1 %share.2 = (f32[256,1024]{1,0:T(8,128)}, f32[256,1024]{1,0:T(8,128)}) custom-call(s32[8]{0:T(128)} %scatter_custom_fusion.table_ref, bf16[512,1024]{1,0:T(8,128)(2,1)} %copy-done, bf16[512,1024]{1,0:T(8,128)(2,1)} %copy-done.1, f32[1024,2048]{1,0:T(8,128)} %refs_8_.1), custom_call_target="tpu_custom_call" | custom-call | flops 300000000 | bytes 1000000 | tf_op jit(solution)/shard_map/share/pallas_call | solution.py:241
  46.1 6.3 %collective-permute-start.9 = (f32[256,1024]{1,0:T(8,128)S(1)}, f32[256,1024]{1,0:T(8,128)S(1)}, u32[]{:S(2)}, u32[]{:S(2)}) collective-permute-start(f32[256,1024]{1,0:T(8,128)S(1)} %copy-done.11), channel_id=1, source_target_pairs={{0,16},{16,0},{32,48},{48,32},{64,80},{80,64},{96,112},{112,96},{1... | collective-permute-start | bytes 3145736 | tf_op jit(solution)/shard_map/ppermute | solution.py:225
  52.4 2.8 %collective-permute-done.9.g1 = f32[256,1024]{1,0:T(8,128)S(1)} collective-permute-done((f32[256,1024]{1,0:T(8,128)S(1)}, f32[256,1024]{1,0:T(8,128)S(1)}, u32[]{:S(2)}, u32[]{:S(2)}) %collective-permute-start.9) | collective-permute-done | bytes 1048608 | tf_op jit(solution)/shard_map/ppermute | solution.py:225
  55.3 1.1 collective-permute-done.8.g0
  56.4 1.2 copy-done.5
  57.6 0.2 fold.1
  57.8 2.6 %collective-permute-start.10 = (f32[128,2048]{1,0:T(8,128)S(1)}, f32[128,2048]{1,0:T(8,128)S(1)}, u32[]{:S(2)}, u32[]{:S(2)}) collective-permute-start(f32[128,2048]{1,0:T(8,128)S(1)} %get-tuple-element.34), channel_id=1, source_target_pairs={{0,32},{16,112},{32,0},{48,80},{64,96},{80,48},{96,64},{112,16},{1... | collective-permute-start | bytes 3145736 | tf_op jit(solution)/shard_map/ppermute | solution.py:225
  60.4 3.1 %gram.1 = (f32[640,128]{1,0:T(8,128)S(1)}, f32[640,128]{1,0:T(8,128)S(1)}) custom-call(s32[1]{0:T(128)} %bitcast.32.core_ref, f32[1024,512]{1,0:T(8,128)S(1)} %get-tuple-element.36.p_ref), custom_call_target="tpu_custom_call" | custom-call | flops 300000000 | bytes 1000000 | tf_op jit(solution)/shard_map/gram/pallas_call | solution.py:207
  63.5 1.6 %collective-permute-done.13 = f32[640,128]{1,0:T(8,128)S(1)} collective-permute-done((f32[640,128]{1,0:T(8,128)S(1)}, f32[640,128]{1,0:T(8,128)S(1)}, u32[]{:S(2)}, u32[]{:S(2)}) %collective-permute-start.13) | collective-permute-done | bytes 327712 | tf_op jit(solution)/shard_map/ppermute | solution.py:225
  65.2 0.9 collective-permute-start.14
  66.1 6.7 %collective-permute-done.10 = f32[128,2048]{1,0:T(8,128)S(1)} collective-permute-done((f32[128,2048]{1,0:T(8,128)S(1)}, f32[128,2048]{1,0:T(8,128)S(1)}, u32[]{:S(2)}, u32[]{:S(2)}) %collective-permute-start.10) | collective-permute-done | bytes 1048608 | tf_op jit(solution)/shard_map/ppermute | solution.py:225
  72.8 0.4 collective-permute-start.11
  73.2 3.0 %collective-permute-done.14 = f32[640,128]{1,0:T(8,128)S(1)} collective-permute-done((f32[640,128]{1,0:T(8,128)S(1)}, f32[640,128]{1,0:T(8,128)S(1)}, u32[]{:S(2)}, u32[]{:S(2)}) %collective-permute-start.14) | collective-permute-done | bytes 327712 | tf_op jit(solution)/shard_map/ppermute | solution.py:225
  76.3 0.4 collective-permute-start.15
  76.7 8.6 %collective-permute-done.15 = f32[640,128]{1,0:T(8,128)S(1)} collective-permute-done((f32[640,128]{1,0:T(8,128)S(1)}, f32[640,128]{1,0:T(8,128)S(1)}, u32[]{:S(2)}, u32[]{:S(2)}) %collective-permute-start.15) | collective-permute-done | bytes 327712 | tf_op jit(solution)/shard_map/ppermute | solution.py:225
  85.3 2.1 %collective-permute-start.16 = (f32[640,128]{1,0:T(8,128)S(1)}, f32[640,128]{1,0:T(8,128)S(1)}, u32[]{:S(2)}, u32[]{:S(2)}) collective-permute-start(f32[640,128]{1,0:T(8,128)S(1)} %add.200), channel_id=1, source_target_pairs={{0,16},{16,0},{32,48},{48,32},{64,80},{80,64},{96,112},{112,96},{1... | collective-permute-start | bytes 983048 | tf_op jit(solution)/shard_map/ppermute | solution.py:225
  87.6 1.0 collective-permute-done.16
  88.8 3.6 %factor.4.refs_0_.w0 = f32[128,640]{1,0:T(8,128)S(1)} custom-call(f32[1280,128]{1,0:T(8,128)S(1)} %pad_maximum_fusion.1.refs_0_.refs_1_.refs_2_.refs_3_), custom_call_target="tpu_custom_call" | custom-call | flops 300000000 | bytes 1000000 | tf_op jit(solution)/shard_map/factor/pallas_call | solution.py:127
  92.4 4.0 %factor.5.refs_1_.w1 = f32[128,640]{1,0:T(8,128)S(1)} custom-call(f32[128,640]{1,0:T(8,128)S(1)} %factor.4.refs_0_.w0, f32[1280,128]{1,0:T(8,128)S(1)} %pad_maximum_fusion.1.refs_0_.refs_1_.refs_2_.refs_3_), custom_call_target="tpu_custom_call" | custom-call | flops 300000000 | bytes 1000000 | tf_op jit(solution)/shard_map/factor/pallas_call | solution.py:127
  96.6 2.6 %collective-permute-start.17 = (f32[128,2048]{1,0:T(8,128)S(1)}, f32[128,2048]{1,0:T(8,128)S(1)}, u32[]{:S(2)}, u32[]{:S(2)}) collective-permute-start(f32[128,2048]{1,0:T(8,128)S(1)} %pad_maximum_fusion.refs_0_), channel_id=1, source_target_pairs={{0,32},{16,112},{32,0},{48,80},{64,96},{80,48},{96,64},{112,16},{1... | collective-permute-start | bytes 3145736 | tf_op jit(solution)/shard_map/ppermute | solution.py:225
  99.1 4.1 %factor.6.refs_2_.w2 = f32[128,640]{1,0:T(8,128)S(1)} custom-call(f32[128,640]{1,0:T(8,128)S(1)} %factor.4.refs_0_.w0, f32[128,640]{1,0:T(8,128)S(1)} %factor.5.refs_1_.w1, f32[1280,128]{1,0:T(8,128)S(1)} %pad_maximum_fusion.1.refs_0_.refs_1_.refs_2_.refs_3_), custom_call_target="tpu_custom_call" | custom-call | flops 300000000 | bytes 1000000 | tf_op jit(solution)/shard_map/factor/pallas_call | solution.py:127
  103.2 4.2 %factor.7.w3 = f32[128,640]{1,0:T(8,128)S(1)} custom-call(f32[128,640]{1,0:T(8,128)S(1)} %factor.4.refs_0_.w0, f32[128,640]{1,0:T(8,128)S(1)} %factor.5.refs_1_.w1, f32[128,640]{1,0:T(8,128)S(1)} %factor.6.refs_2_.w2, f32[1280,128]{1,0:T(8,128)S(1)} %pad_maximum_fusion.1.refs_0_.refs_1_.refs_2_.refs_3_), custom_call_target="tpu_custom_call" | custom-call | flops 300000000 | bytes 1000000 | tf_op jit(solution)/shard_map/factor/pallas_call | solution.py:127
  107.5 3.0 %prepare.1 = (f32[512,512]{1,0:T(8,128)}, bf16[512,512]{1,0:T(8,128)(2,1)S(1)}, bf16[512,512]{1,0:T(8,128)(2,1)S(1)}, bf16[1024,512]{1,0:T(8,128)(2,1)S(1)}, bf16[1024,512]{1,0:T(8,128)(2,1)S(1)}) custom-call(f32[128,640]{1,0:T(8,128)S(1)} %factor.4.refs_0_.w0, f32[128,640]{1,0:T(8,128)S(1)} %factor.5.refs_1_.w1, f32[128,640]{1,0:T(8,128)S(1)} %factor.6.refs_2_.w2, ...), custom_call_target="tpu_custom_call" | custom-call | flops 300000000 | bytes 1000000 | tf_op jit(solution)/shard_map/prepare/pallas_call | solution.py:298
  110.5 1.0 copy-done.2
  111.5 1.0 copy-done.3
  112.5 0.8 copy-done.6
  113.3 0.8 copy-done.7
  114.1 0.5 collective-permute-start.19
  114.6 0.6 stack.167.table_ref
  115.1 1.8 %collective-permute-done.19.refs_3_ = f32[128,2048]{1,0:T(8,128)} collective-permute-done((f32[128,2048]{1,0:T(8,128)S(1)}, f32[128,2048]{1,0:T(8,128)}, u32[]{:S(2)}, u32[]{:S(2)}) %collective-permute-start.19) | collective-permute-done | bytes 1048608 | tf_op jit(solution)/shard_map/ppermute | solution.py:225
  117.0 15.7 %finish.1 = (f32[512,2048]{1,0:T(8,128)}, f32[1024,2048]{1,0:T(8,128)}) custom-call(s32[8]{0:T(128)} %stack.167.table_ref, f32[128,2048]{1,0:T(8,128)} %copy-done.8, f32[128,2048]{1,0:T(8,128)} %copy-done.9, f32[128,2048]{1,0:T(8,128)} %copy-done.10, f32[128,2048]{1,0:T(8,128)} %collective-permute-done.19.refs_3_, bf16[512,512]{1,0:T(8,128)(2,1)} %copy-done.6, ...), custom_call_target="tpu_custom_call" | custom-call | tf_op jit(solution)/shard_map/finish/pallas_call | solution.py:326
  (48 shorter events, 1.3 us)
Async XLA Ops:
  1.5 4.1 %collective-permute-start = (f32[64,256]{1,0:T(8,128)S(1)}, f32[64,256]{1,0:T(8,128)S(1)}, u32[]{:S(2)}, u32[]{:S(2)}) collective-permute-start(f32[64,256]{1,0:T(8,128)S(1)} %get-tuple-element.54), channel_id=1, source_target_pairs={{0,1},{1,0},{2,3},{3,2},{4,5},{5,4},{6,7},{7,6},{8,9},{9,8},{10,11... | collective-permute-start | bytes 196616 | tf_op jit(solution)/shard_map/ppermute | solution.py:159
  3.7 4.7 %collective-permute-start.4 = (f32[64,256]{1,0:T(8,128)S(1)}, f32[64,256]{1,0:T(8,128)S(1)}, u32[]{:S(2)}, u32[]{:S(2)}) collective-permute-start(f32[64,256]{1,0:T(8,128)S(1)} %get-tuple-element.53), channel_id=1, source_target_pairs={{0,3},{1,2},{2,1},{3,0},{4,7},{5,6},{6,5},{7,4},{8,11},{9,10},{10,... | collective-permute-start | bytes 196616 | tf_op jit(solution)/shard_map/ppermute | solution.py:159
  5.6 5.1 %collective-permute-start.1 = (f32[128,256]{1,0:T(8,128)S(1)}, f32[128,256]{1,0:T(8,128)S(1)}, u32[]{:S(2)}, u32[]{:S(2)}) collective-permute-start(f32[128,256]{1,0:T(8,128)S(1)} %pad_maximum_fusion.6), channel_id=1, source_target_pairs={{0,3},{1,2},{2,1},{3,0},{4,7},{5,6},{6,5},{7,4},{8,11},{9,10},{10,... | collective-permute-start | bytes 393224 | tf_op jit(solution)/shard_map/ppermute | solution.py:159
  8.4 4.1 %collective-permute-start.5 = (f32[128,256]{1,0:T(8,128)S(1)}, f32[128,256]{1,0:T(8,128)S(1)}, u32[]{:S(2)}, u32[]{:S(2)}) collective-permute-start(f32[128,256]{1,0:T(8,128)S(1)} %pad_maximum_fusion.7), channel_id=1, source_target_pairs={{0,1},{1,0},{2,3},{3,2},{4,5},{5,4},{6,7},{7,6},{8,9},{9,8},{10,11... | collective-permute-start | bytes 393224 | tf_op jit(solution)/shard_map/ppermute | solution.py:159
  10.8 7.2 %collective-permute-start.2 = (f32[256,256]{1,0:T(8,128)S(1)}, f32[256,256]{1,0:T(8,128)S(1)}, u32[]{:S(2)}, u32[]{:S(2)}) collective-permute-start(f32[256,256]{1,0:T(8,128)S(1)} %pad_maximum_fusion.4), channel_id=1, source_target_pairs={{0,4},{1,5},{2,6},{3,7},{4,0},{5,1},{6,2},{7,3},{8,12},{9,13},{10,... | collective-permute-start | bytes 786440 | tf_op jit(solution)/shard_map/ppermute | solution.py:159
  12.5 7.7 %collective-permute-start.6 = (f32[256,256]{1,0:T(8,128)S(1)}, f32[256,256]{1,0:T(8,128)S(1)}, u32[]{:S(2)}, u32[]{:S(2)}) collective-permute-start(f32[256,256]{1,0:T(8,128)S(1)} %pad_maximum_fusion.5), channel_id=1, source_target_pairs={{0,12},{1,13},{2,14},{3,15},{4,8},{5,9},{6,10},{7,11},{8,4},{9,5},... | collective-permute-start | bytes 786440 | tf_op jit(solution)/shard_map/ppermute | solution.py:159
  18.0 9.6 %collective-permute-start.3 = (f32[512,256]{1,0:T(8,128)S(1)}, f32[512,256]{1,0:T(8,128)S(1)}, u32[]{:S(2)}, u32[]{:S(2)}) collective-permute-start(f32[512,256]{1,0:T(8,128)S(1)} %pad_maximum_fusion.2.refs_0_), channel_id=1, source_target_pairs={{0,12},{1,13},{2,14},{3,15},{4,8},{5,9},{6,10},{7,11},{8,4},{9,5},... | collective-permute-start | bytes 1572872 | tf_op jit(solution)/shard_map/ppermute | solution.py:159
  20.2 8.4 %collective-permute-start.7 = (f32[512,256]{1,0:T(8,128)S(1)}, f32[512,256]{1,0:T(8,128)S(1)}, u32[]{:S(2)}, u32[]{:S(2)}) collective-permute-start(f32[512,256]{1,0:T(8,128)S(1)} %pad_maximum_fusion.3.refs_2_), channel_id=1, source_target_pairs={{0,4},{1,5},{2,6},{3,7},{4,0},{5,1},{6,2},{7,3},{8,12},{9,13},{10,... | collective-permute-start | bytes 1572872 | tf_op jit(solution)/shard_map/ppermute | solution.py:159
  30.1 1.0 copy-start
  31.1 1.0 copy-start.1
  38.9 7.1 %copy-start.11 = (f32[256,1024]{1,0:T(8,128)S(1)}, f32[256,1024]{1,0:T(8,128)}, u32[]{:S(2)}) copy-start(f32[256,1024]{1,0:T(8,128)} %get-tuple-element.32) | copy-start | bytes 3145732
  38.9 17.4 %copy-start.4 = (f32[256,1024]{1,0:T(8,128)S(1)}, f32[256,1024]{1,0:T(8,128)}, u32[]{:S(2)}) copy-start(f32[256,1024]{1,0:T(8,128)} %get-tuple-element.30.k1) | copy-start | bytes 3145732
  46.1 9.2 %collective-permute-start.9 = (f32[256,1024]{1,0:T(8,128)S(1)}, f32[256,1024]{1,0:T(8,128)S(1)}, u32[]{:S(2)}, u32[]{:S(2)}) collective-permute-start(f32[256,1024]{1,0:T(8,128)S(1)} %copy-done.11), channel_id=1, source_target_pairs={{0,16},{16,0},{32,48},{48,32},{64,80},{80,64},{96,112},{112,96},{1... | collective-permute-start | bytes 3145736 | tf_op jit(solution)/shard_map/ppermute | solution.py:225
  52.4 4.0 %collective-permute-start.8 = (f32[256,1024]{1,0:T(8,128)}, f32[256,1024]{1,0:T(8,128)S(1)}, u32[]{:S(2)}, u32[]{:S(2)}) collective-permute-start(f32[256,1024]{1,0:T(8,128)} %get-tuple-element.31), channel_id=1, source_target_pairs={{0,16},{16,0},{32,48},{48,32},{64,80},{80,64},{96,112},{112,96},{1... | collective-permute-start | bytes 3145736 | tf_op jit(solution)/shard_map/ppermute | solution.py:225
  56.4 1.2 copy-start.5
  57.8 14.9 %collective-permute-start.10 = (f32[128,2048]{1,0:T(8,128)S(1)}, f32[128,2048]{1,0:T(8,128)S(1)}, u32[]{:S(2)}, u32[]{:S(2)}) collective-permute-start(f32[128,2048]{1,0:T(8,128)S(1)} %get-tuple-element.34), channel_id=1, source_target_pairs={{0,32},{16,112},{32,0},{48,80},{64,96},{80,48},{96,64},{112,16},{1... | collective-permute-start | bytes 3145736 | tf_op jit(solution)/shard_map/ppermute | solution.py:225
  63.4 1.7 %collective-permute-start.13 = (f32[640,128]{1,0:T(8,128)S(1)}, f32[640,128]{1,0:T(8,128)S(1)}, u32[]{:S(2)}, u32[]{:S(2)}) collective-permute-start(f32[640,128]{1,0:T(8,128)S(1)} %get-tuple-element.38), channel_id=1, source_target_pairs={{0,16},{16,0},{32,48},{48,32},{64,80},{80,64},{96,112},{112,96},{1... | collective-permute-start | bytes 983048 | tf_op jit(solution)/shard_map/ppermute | solution.py:225
  65.2 11.1 %collective-permute-start.14 = (f32[640,128]{1,0:T(8,128)S(1)}, f32[640,128]{1,0:T(8,128)S(1)}, u32[]{:S(2)}, u32[]{:S(2)}) collective-permute-start(f32[640,128]{1,0:T(8,128)S(1)} %add.198), channel_id=1, source_target_pairs={{0,32},{16,112},{32,0},{48,80},{64,96},{80,48},{96,64},{112,16},{1... | collective-permute-start | bytes 983048 | tf_op jit(solution)/shard_map/ppermute | solution.py:225
  72.8 14.6 %collective-permute-start.11 = (f32[64,2048]{1,0:T(8,128)S(1)}, f32[64,2048]{1,0:T(8,128)S(1)}, u32[]{:S(2)}, u32[]{:S(2)}) collective-permute-start(f32[64,2048]{1,0:T(8,128)S(1)} %slice_add_fusion), channel_id=1, source_target_pairs={{0,96},{16,48},{32,64},{48,16},{64,32},{80,112},{96,0},{112,80},{1... | collective-permute-start | bytes 1572872 | tf_op jit(solution)/shard_map/ppermute | solution.py:225
  76.3 9.0 %collective-permute-start.15 = (f32[640,128]{1,0:T(8,128)S(1)}, f32[640,128]{1,0:T(8,128)S(1)}, u32[]{:S(2)}, u32[]{:S(2)}) collective-permute-start(f32[640,128]{1,0:T(8,128)S(1)} %add.199), channel_id=1, source_target_pairs={{0,96},{16,48},{32,64},{48,16},{64,32},{80,112},{96,0},{112,80},{1... | collective-permute-start | bytes 983048 | tf_op jit(solution)/shard_map/ppermute | solution.py:225
  85.3 3.3 %collective-permute-start.16 = (f32[640,128]{1,0:T(8,128)S(1)}, f32[640,128]{1,0:T(8,128)S(1)}, u32[]{:S(2)}, u32[]{:S(2)}) collective-permute-start(f32[640,128]{1,0:T(8,128)S(1)} %add.200), channel_id=1, source_target_pairs={{0,16},{16,0},{32,48},{48,32},{64,80},{80,64},{96,112},{112,96},{1... | collective-permute-start | bytes 983048 | tf_op jit(solution)/shard_map/ppermute | solution.py:225
  87.5 8.9 %collective-permute-start.12 = (f32[64,2048]{1,0:T(8,128)S(1)}, f32[64,2048]{1,0:T(8,128)S(1)}, u32[]{:S(2)}, u32[]{:S(2)}) collective-permute-start(f32[64,2048]{1,0:T(8,128)S(1)} %fusion), channel_id=1, source_target_pairs={{0,96},{16,48},{32,64},{48,16},{64,32},{80,112},{96,0},{112,80},{1... | collective-permute-start | bytes 1572872 | tf_op jit(solution)/shard_map/ppermute | solution.py:225
  96.5 20.4 %copy-start.8 = (f32[128,2048]{1,0:T(8,128)}, f32[128,2048]{1,0:T(8,128)S(1)}, u32[]{:S(2)}) copy-start(f32[128,2048]{1,0:T(8,128)S(1)} %pad_maximum_fusion.refs_0_) | copy-start | bytes 3145732
  96.6 17.5 %collective-permute-start.17 = (f32[128,2048]{1,0:T(8,128)S(1)}, f32[128,2048]{1,0:T(8,128)S(1)}, u32[]{:S(2)}, u32[]{:S(2)}) collective-permute-start(f32[128,2048]{1,0:T(8,128)S(1)} %pad_maximum_fusion.refs_0_), channel_id=1, source_target_pairs={{0,32},{16,112},{32,0},{48,80},{64,96},{80,48},{96,64},{112,16},{1... | collective-permute-start | bytes 3145736 | tf_op jit(solution)/shard_map/ppermute | solution.py:225
  99.1 16.0 %collective-permute-start.18 = (f32[128,2048]{1,0:T(8,128)S(1)}, f32[128,2048]{1,0:T(8,128)S(1)}, u32[]{:S(2)}, u32[]{:S(2)}) collective-permute-start(f32[128,2048]{1,0:T(8,128)S(1)} %pad_maximum_fusion.refs_0_), channel_id=1, source_target_pairs={{0,16},{16,0},{32,48},{48,32},{64,80},{80,64},{96,112},{112,96},{1... | collective-permute-start | bytes 3145736 | tf_op jit(solution)/shard_map/ppermute | solution.py:225
  110.5 1.0 copy-start.2
  111.5 1.0 copy-start.3
  112.5 0.8 copy-start.6
  113.3 0.8 copy-start.7
  114.1 2.9 %copy-start.9 = (f32[128,2048]{1,0:T(8,128)}, f32[128,2048]{1,0:T(8,128)S(1)}, u32[]{:S(2)}) copy-start(f32[128,2048]{1,0:T(8,128)S(1)} %collective-permute-done.17.refs_1_) | copy-start | bytes 3145732
  114.1 2.9 %collective-permute-start.19 = (f32[128,2048]{1,0:T(8,128)S(1)}, f32[128,2048]{1,0:T(8,128)}, u32[]{:S(2)}, u32[]{:S(2)}) collective-permute-start(f32[128,2048]{1,0:T(8,128)S(1)} %collective-permute-done.17.refs_1_), channel_id=1, source_target_pairs={{0,16},{16,0},{32,48},{48,32},{64,80},{80,64},{96,112},{112,96},{1... | collective-permute-start | bytes 3145736 | tf_op jit(solution)/shard_map/ppermute | solution.py:225
  115.1 1.9 %copy-start.10 = (f32[128,2048]{1,0:T(8,128)}, f32[128,2048]{1,0:T(8,128)S(1)}, u32[]{:S(2)}) copy-start(f32[128,2048]{1,0:T(8,128)S(1)} %collective-permute-done.18.refs_2_) | copy-start | bytes 3145732
